TPU v7x, 128 devices: a whole 4x4x4 slice. The times are simulated.
128 devices in a mesh: nodes: 32 (over y, z, core), rel: 4 (over x).
Axes of the slice: x: 4, y: 4, z: 4, core: 2. Of those that a mesh axis runs over, the one named last changes fastest.
Arguments:
- grad_out: bfloat16 [147456, 1024], P('nodes'), may hold values from -6 to 6
- paper_feat: bfloat16 [147456, 768], P('nodes'), may hold values from -6 to 6
- saved_agg: bfloat16 [4, 147456, 256], P('rel', 'nodes'), may hold values from -6 to 6
- rel_weight: bfloat16 [4, 256, 1024], P('rel'), may hold values from -0.375 to 0.375
- slot_paper: int32 [32, 4, 32, 128], P('nodes', 'rel'), may hold values from 0 to 4607, as said below
- slot_author: int32 [32, 4, 32, 128], P('nodes', 'rel'), may hold values from 0 to 2047, as said below
- block_count: int32 [32, 4, 32], P('nodes', 'rel'), may hold values from 4 to 128, as said below
Outputs:
- grad_author: float32 [65536, 256], P(('nodes', 'rel'))
- grad_rel: float32 [4, 256, 1024], P('rel', 'nodes')
- grad_self: float32 [768, 1024], P('nodes', 'rel')
Inputs may be any that keep to these rules, and one draw needn't show every extreme that they name: `slot_paper`: every draw uses the first and the last paper of a shard. `slot_author`: rows repeat across slots and blocks. `block_count`: live slots are counted from slot 0; some blocks are full.
All inputs are finite; a program needn't handle non-finite values.
Results may differ from a plain program's by a relative error of at most 0.0065.
Values may be sent and summed in bfloat16 or wider, within the bound.
A program may use at most 128 MiB of HBM per device.

v0:
```python
import math

import jax
import jax.numpy as jnp
from jax import lax
from jax.sharding import PartitionSpec as P

AUTH_DEV = 512


def slot_weights(values_shape, counts):
    slot_total = values_shape[1]
    alive_mask = (jnp.arange(slot_total, dtype=jnp.int32)[None, :] < counts[:, None]).astype(
        jnp.float32
    )
    return lax.rsqrt(counts.astype(jnp.float32))[:, None] * alive_mask


def pick_rows(table_bf, indices):
    edge_total = indices.shape[0]
    table_rows = table_bf.shape[0]
    step_rows = math.gcd(edge_total, 512)
    grouped_idx = indices.reshape(edge_total // step_rows, step_rows)
    column_ids = jnp.arange(table_rows, dtype=jnp.int32)

    def one_block(block_idx):
        onehot = (block_idx[:, None] == column_ids[None, :]).astype(jnp.bfloat16)
        return jnp.dot(onehot, table_bf, preferred_element_type=jnp.float32).astype(jnp.bfloat16)

    picked = lax.map(one_block, grouped_idx)
    return picked.reshape(edge_total, table_bf.shape[1])


def rows_sum(values_bf, weights, targets, row_total):
    edge_total, width = values_bf.shape
    scaled = values_bf.astype(jnp.float32) * weights[:, None]
    high_part = scaled.astype(jnp.bfloat16)
    low_part = (scaled - high_part.astype(jnp.float32)).astype(jnp.bfloat16)
    step_rows = math.gcd(edge_total, 512)
    block_total = edge_total // step_rows
    high_blocks = high_part.reshape(block_total, step_rows, width)
    low_blocks = low_part.reshape(block_total, step_rows, width)
    target_blocks = targets.reshape(block_total, step_rows)
    row_ids = jnp.arange(row_total, dtype=jnp.int32)

    def add_block(running, operands):
        high_rows, low_rows, block_targets = operands
        onehot = (block_targets[:, None] == row_ids[None, :]).astype(jnp.bfloat16)
        contract = (((0,), (0,)), ((), ()))
        running = running + lax.dot_general(
            onehot, high_rows, contract, preferred_element_type=jnp.float32
        )
        running = running + lax.dot_general(
            onehot, low_rows, contract, preferred_element_type=jnp.float32
        )
        return (running, None)

    start = jnp.zeros((row_total, width), jnp.float32)
    total, _ = lax.scan(add_block, start, (high_blocks, low_blocks, target_blocks))
    return total


def on_device(grad_out, paper_feat, saved_agg, rel_weight, slot_paper, slot_author, block_count):
    node_count = lax.axis_size("nodes")
    rel_count = lax.axis_size("rel")
    author_w = rel_weight.shape[1]
    hidden_w = grad_out.shape[1]
    col_width = hidden_w // rel_count
    group_rows = AUTH_DEV * rel_count
    weight = rel_weight[0]
    aggregate = saved_agg[0]
    papers = slot_paper[0, 0]
    authors = slot_author[0, 0]
    counts = block_count[0, 0]
    blocks, slot_total = papers.shape
    back_rows = lax.dot_general(
        grad_out, weight, (((1,), (1,)), ((), ())), preferred_element_type=jnp.float32
    )
    back_bf = back_rows.astype(jnp.bfloat16)
    messages = pick_rows(back_bf, papers.reshape(-1)).reshape(blocks, slot_total, author_w)
    arrived, arrived_rows, arrived_count = (
        lax.all_to_all(messages, "nodes", split_axis=0, concat_axis=0, tiled=True),
        lax.all_to_all(authors, "nodes", split_axis=0, concat_axis=0, tiled=True),
        lax.all_to_all(counts, "nodes", split_axis=0, concat_axis=0, tiled=True),
    )
    weights = slot_weights(arrived_rows.shape, arrived_count)
    grouped = rows_sum(
        arrived.reshape(-1, author_w), weights.reshape(-1), arrived_rows.reshape(-1), group_rows
    )
    grad_author = lax.psum_scatter(grouped, "rel", scatter_dimension=0, tiled=True)
    column_start = lax.axis_index("rel") * col_width
    grad_cols = lax.dynamic_slice_in_dim(grad_out, column_start, col_width, 1)
    rel_share = author_w // node_count
    self_share = paper_feat.shape[1] // node_count
    rel_term = lax.dot_general(
        aggregate, grad_out, (((0,), (0,)), ((), ())), preferred_element_type=jnp.float32
    )
    self_term = lax.dot_general(
        paper_feat, grad_cols, (((0,), (0,)), ((), ())), preferred_element_type=jnp.float32
    )
    rel_total, self_total = lax.psum((rel_term, self_term), "nodes")
    node_index = lax.axis_index("nodes")
    grad_rel = lax.dynamic_slice_in_dim(rel_total, node_index * rel_share, rel_share, 0)
    grad_self = lax.dynamic_slice_in_dim(self_total, node_index * self_share, self_share, 0)
    return (grad_author, grad_rel[None], grad_self)


def solution(mesh):
    return jax.shard_map(
        on_device,
        mesh=mesh,
        in_specs=(
            P("nodes", None),
            P("nodes", None),
            P("rel", "nodes", None),
            P("rel", None, None),
            P("nodes", "rel", None, None),
            P("nodes", "rel", None, None),
            P("nodes", "rel", None),
        ),
        out_specs=(P(("nodes", "rel"), None), P("rel", "nodes", None), P("nodes", "rel")),
        check_vma=False,
    )
```

profile of v0, /device:TPU:0, one launch (start us, length us, event | category | flops | bytes accessed | tf_op | source)
XLA Modules:
  0.0 207.3 jit_solution(9823896879667837094)
XLA Ops:
  8.0 1.5 copy.16
  9.5 8.4 %all-to-all-start.2 = ((s32[32,1,1]{2,1,0:T(1,128)}), s32[32,1,1]{2,1,0:T(1,128)S(1)}, u32[]{:S(2)}, u32[]{:S(2)}) async-start(s32[32,1,1]{2,1,0:T(1,128)} %copy.16), calls=%async_computation.2 | async-start | bytes 32768 | tf_op jit(solution)/shard_map/all_to_all | solution.py:84
  17.9 0.7 reshape_reshape_squeeze.3
  18.7 7.8 %convolution_convert_fusion = bf16[4608,256]{1,0:T(8,128)(2,1)} fusion(bf16[4608,1024]{1,0:T(8,128)(2,1)} %param.11, bf16[1,256,1024]{2,1,0:T(8,128)(2,1)} %param.14), kind=kOutput, calls=%fused_computation.23 | convolution fusion | flops 2417098752 | bytes 12320768 | tf_op jit(solution)/shard_map/dot_general | solution.py:76
  26.5 7.4 %all-to-all-start = ((s32[32,1,128]{2,1,0:T(1,128)}), s32[32,1,128]{2,1,0:T(1,128)S(1)}, u32[]{:S(2)}, u32[]{:S(2)}) async-start(s32[32,1,128]{2,1,0:T(1,128)} %bitcast), calls=%async_computation | async-start | bytes 32768 | tf_op jit(solution)/shard_map/all_to_all | solution.py:83
  33.8 32.6 %while.22 = (s32[]{:T(128)}, bf16[8,512,256]{2,1,0:T(8,128)(2,1)}, s32[8,512]{1,0:T(8,128)S(1)}, bf16[4608,256]{1,0:T(8,128)(2,1)}, s32[]{:T(128)}) while((s32[]{:T(128)}, bf16[8,512,256]{2,1,0:T(8,128)(2,1)}, s32[8,512]{1,0:T(8,128)S(1)}, bf16[4608,256]{1,0:T(8,128)(2,1)}, s32[]{:T(128)}) %tuple.46), condition=%wide.region_1.2_spmd.clone, body=%wide.region_0.1_spmd.clone.sunk | while | flops 1210449920 | bytes 2628161 | solution.py:30
  33.9 4.1 %fusion.44 = bf16[8,512,256]{2,1,0:T(8,128)(2,1)} fusion(bf16[8,512,256]{2,1,0:T(8,128)(2,1)} %get-tuple-element.187, s32[]{:T(128)} %get-tuple-element.186, bf16[4608,256]{1,0:T(8,128)(2,1)} %get-tuple-element.194, s32[512]{0:T(512)S(1)} %bitcast.59), kind=kOutput, calls=%fused_computation.7.clone.1 | convolution fusion | flops 1210449920 | bytes 2624000 | tf_op jit(solution)/shard_map/while/body/eval_jaxpr/dot_general | solution.py:28
  38.0 4.1 %fusion.44 = bf16[8,512,256]{2,1,0:T(8,128)(2,1)} fusion(bf16[8,512,256]{2,1,0:T(8,128)(2,1)} %get-tuple-element.187, s32[]{:T(128)} %get-tuple-element.186, bf16[4608,256]{1,0:T(8,128)(2,1)} %get-tuple-element.194, s32[512]{0:T(512)S(1)} %bitcast.59), kind=kOutput, calls=%fused_computation.7.clone.1 | convolution fusion | flops 1210449920 | bytes 2624000 | tf_op jit(solution)/shard_map/while/body/eval_jaxpr/dot_general | solution.py:28
  42.0 4.1 %fusion.44 = bf16[8,512,256]{2,1,0:T(8,128)(2,1)} fusion(bf16[8,512,256]{2,1,0:T(8,128)(2,1)} %get-tuple-element.187, s32[]{:T(128)} %get-tuple-element.186, bf16[4608,256]{1,0:T(8,128)(2,1)} %get-tuple-element.194, s32[512]{0:T(512)S(1)} %bitcast.59), kind=kOutput, calls=%fused_computation.7.clone.1 | convolution fusion | flops 1210449920 | bytes 2624000 | tf_op jit(solution)/shard_map/while/body/eval_jaxpr/dot_general | solution.py:28
  46.1 4.1 %fusion.44 = bf16[8,512,256]{2,1,0:T(8,128)(2,1)} fusion(bf16[8,512,256]{2,1,0:T(8,128)(2,1)} %get-tuple-element.187, s32[]{:T(128)} %get-tuple-element.186, bf16[4608,256]{1,0:T(8,128)(2,1)} %get-tuple-element.194, s32[512]{0:T(512)S(1)} %bitcast.59), kind=kOutput, calls=%fused_computation.7.clone.1 | convolution fusion | flops 1210449920 | bytes 2624000 | tf_op jit(solution)/shard_map/while/body/eval_jaxpr/dot_general | solution.py:28
  50.2 4.1 %fusion.44 = bf16[8,512,256]{2,1,0:T(8,128)(2,1)} fusion(bf16[8,512,256]{2,1,0:T(8,128)(2,1)} %get-tuple-element.187, s32[]{:T(128)} %get-tuple-element.186, bf16[4608,256]{1,0:T(8,128)(2,1)} %get-tuple-element.194, s32[512]{0:T(512)S(1)} %bitcast.59), kind=kOutput, calls=%fused_computation.7.clone.1 | convolution fusion | flops 1210449920 | bytes 2624000 | tf_op jit(solution)/shard_map/while/body/eval_jaxpr/dot_general | solution.py:28
  54.3 4.1 %fusion.44 = bf16[8,512,256]{2,1,0:T(8,128)(2,1)} fusion(bf16[8,512,256]{2,1,0:T(8,128)(2,1)} %get-tuple-element.187, s32[]{:T(128)} %get-tuple-element.186, bf16[4608,256]{1,0:T(8,128)(2,1)} %get-tuple-element.194, s32[512]{0:T(512)S(1)} %bitcast.59), kind=kOutput, calls=%fused_computation.7.clone.1 | convolution fusion | flops 1210449920 | bytes 2624000 | tf_op jit(solution)/shard_map/while/body/eval_jaxpr/dot_general | solution.py:28
  58.4 4.1 %fusion.44 = bf16[8,512,256]{2,1,0:T(8,128)(2,1)} fusion(bf16[8,512,256]{2,1,0:T(8,128)(2,1)} %get-tuple-element.187, s32[]{:T(128)} %get-tuple-element.186, bf16[4608,256]{1,0:T(8,128)(2,1)} %get-tuple-element.194, s32[512]{0:T(512)S(1)} %bitcast.59), kind=kOutput, calls=%fused_computation.7.clone.1 | convolution fusion | flops 1210449920 | bytes 2624000 | tf_op jit(solution)/shard_map/while/body/eval_jaxpr/dot_general | solution.py:28
  62.4 4.1 %fusion.44 = bf16[8,512,256]{2,1,0:T(8,128)(2,1)} fusion(bf16[8,512,256]{2,1,0:T(8,128)(2,1)} %get-tuple-element.187, s32[]{:T(128)} %get-tuple-element.186, bf16[4608,256]{1,0:T(8,128)(2,1)} %get-tuple-element.194, s32[512]{0:T(512)S(1)} %bitcast.59), kind=kOutput, calls=%fused_computation.7.clone.1 | convolution fusion | flops 1210449920 | bytes 2624000 | tf_op jit(solution)/shard_map/while/body/eval_jaxpr/dot_general | solution.py:28
  66.5 7.5 %all-to-all-start.1 = ((bf16[32,128,256]{2,1,0:T(8,128)(2,1)}), bf16[32,128,256]{2,1,0:T(8,128)(2,1)}, u32[]{:S(2)}, u32[]{:S(2)}) async-start(bf16[32,128,256]{2,1,0:T(8,128)(2,1)} %bitcast.56), calls=%async_computation.1 | async-start | bytes 4194304 | tf_op jit(solution)/shard_map/all_to_all | solution.py:82
  74.1 6.7 %fusion.28 = f32[768,256]{0,1:T(8,128)} fusion(bf16[4608,768]{1,0:T(8,128)(2,1)} %param.12, bf16[4608,1024]{1,0:T(8,128)(2,1)} %param.11, s32[]{:T(128)S(6)} %select_n.10), kind=kOutput, calls=%fused_computation.32 | convolution fusion | flops 1811939328 | bytes 10223620 | tf_op jit(solution)/shard_map/dot_general | solution.py:98
  80.7 7.3 %fusion.24 = f32[256,1024]{1,0:T(8,128)} fusion(bf16[4608,1024]{1,0:T(8,128)(2,1)} %param.11, bf16[1,4608,256]{2,1,0:T(8,128)(2,1)S(1)} %copy-done), kind=kOutput, calls=%fused_computation.28 | convolution fusion | flops 2415919104 | bytes 12845056 | tf_op jit(solution)/shard_map/dot_general | solution.py:95
  88.1 0.2 reduce-scatter.2.cloned.1.call-start
  88.3 0.7 reduce.1
  89.0 0.1 lt.40
  89.1 0.1 copy.17
  89.2 0.1 copy.18
  89.2 0.1 bitcast_select_fusion
  89.3 0.5 broadcast.33
  89.9 0.7 reduce.4
  90.6 12.4 %all-to-all-done.1 = bf16[32,128,256]{2,1,0:T(8,128)(2,1)} async-done(((bf16[32,128,256]{2,1,0:T(8,128)(2,1)}), bf16[32,128,256]{2,1,0:T(8,128)(2,1)}, u32[]{:S(2)}, u32[]{:S(2)}) %all-to-all-start.1) | async-done | bytes 2097184 | tf_op jit(solution)/shard_map/all_to_all | solution.py:82
  102.9 3.6 %fusion.23 = (bf16[8,512,256]{2,1,0:T(8,128)(2,1)}, bf16[8,512,256]{2,1,0:T(8,128)(2,1)}) fusion(f32[8,512]{1,0:T(8,128)S(1)} %bitcast_select_fusion, bf16[8,512,256]{2,1,0:T(8,128)(2,1)} %bitcast.43), kind=kLoop, calls=%fused_computation.27 | loop fusion | flops 6291456 | bytes 6307840 | tf_op jit(solution)/shard_map/convert_element_type | solution.py:38
  106.5 54.0 %while.23 = (s32[]{:T(128)}, f32[2048,256]{1,0:T(8,128)}, s32[8,512]{1,0:T(8,128)S(1)}, bf16[8,512,256]{2,1,0:T(8,128)(2,1)}, bf16[8,512,256]{2,1,0:T(8,128)(2,1)}, /*index=5*/s32[]{:T(128)}, s32[]{:T(128)}) while((s32[]{:T(128)}, f32[2048,256]{1,0:T(8,128)}, s32[8,512]{1,0:T(8,128)S(1)}, bf16[8,512,256]{2,1,0:T(8,128)(2,1)}, ...), condition=%wide.region_3.4_spmd.clone, body=%wide.region_2.3_spmd.clone.sunk | while | flops 1077411840 | bytes 8922203 | solution.py:59
  106.5 2.4 %fusion.47 = f32[2048,256]{1,0:T(8,128)S(1)} fusion(f32[2048,256]{1,0:T(8,128)} %get-tuple-element.204, s32[512]{0:T(512)S(1)} %bitcast.57, pred[]{:T(512)S(6)} %compare.3, bf16[8,512,256]{2,1,0:T(8,128)(2,1)} %get-tuple-element.213, s32[]{:T(128)} %get-tuple-element.203), kind=kOutput, calls=%fused_computation.12.clone.1 | convolution fusion | flops 538968064 | bytes 4459009 | tf_op jit(solution)/shard_map/while/body/eval_jaxpr/dot_general | solution.py:50
  108.9 3.7 %fusion.48 = f32[2048,256]{1,0:T(8,128)} fusion(f32[2048,256]{1,0:T(8,128)S(1)} %fusion.47, s32[512]{0:T(512)S(1)} %bitcast.58, bf16[8,512,256]{2,1,0:T(8,128)(2,1)} %get-tuple-element.214, s32[]{:T(128)} %get-tuple-element.203), kind=kOutput, calls=%fused_computation.13.clone.1 | convolution fusion | flops 538443776 | bytes 4459008 | tf_op jit(solution)/shard_map/while/body/eval_jaxpr/dot_general | solution.py:53
  112.6 3.1 %fusion.47 = f32[2048,256]{1,0:T(8,128)S(1)} fusion(f32[2048,256]{1,0:T(8,128)} %get-tuple-element.204, s32[512]{0:T(512)S(1)} %bitcast.57, pred[]{:T(512)S(6)} %compare.3, bf16[8,512,256]{2,1,0:T(8,128)(2,1)} %get-tuple-element.213, s32[]{:T(128)} %get-tuple-element.203), kind=kOutput, calls=%fused_computation.12.clone.1 | convolution fusion | flops 538968064 | bytes 4459009 | tf_op jit(solution)/shard_map/while/body/eval_jaxpr/dot_general | solution.py:50
  115.8 3.7 %fusion.48 = f32[2048,256]{1,0:T(8,128)} fusion(f32[2048,256]{1,0:T(8,128)S(1)} %fusion.47, s32[512]{0:T(512)S(1)} %bitcast.58, bf16[8,512,256]{2,1,0:T(8,128)(2,1)} %get-tuple-element.214, s32[]{:T(128)} %get-tuple-element.203), kind=kOutput, calls=%fused_computation.13.clone.1 | convolution fusion | flops 538443776 | bytes 4459008 | tf_op jit(solution)/shard_map/while/body/eval_jaxpr/dot_general | solution.py:53
  119.5 3.1 %fusion.47 = f32[2048,256]{1,0:T(8,128)S(1)} fusion(f32[2048,256]{1,0:T(8,128)} %get-tuple-element.204, s32[512]{0:T(512)S(1)} %bitcast.57, pred[]{:T(512)S(6)} %compare.3, bf16[8,512,256]{2,1,0:T(8,128)(2,1)} %get-tuple-element.213, s32[]{:T(128)} %get-tuple-element.203), kind=kOutput, calls=%fused_computation.12.clone.1 | convolution fusion | flops 538968064 | bytes 4459009 | tf_op jit(solution)/shard_map/while/body/eval_jaxpr/dot_general | solution.py:50
  122.6 3.7 %fusion.48 = f32[2048,256]{1,0:T(8,128)} fusion(f32[2048,256]{1,0:T(8,128)S(1)} %fusion.47, s32[512]{0:T(512)S(1)} %bitcast.58, bf16[8,512,256]{2,1,0:T(8,128)(2,1)} %get-tuple-element.214, s32[]{:T(128)} %get-tuple-element.203), kind=kOutput, calls=%fused_computation.13.clone.1 | convolution fusion | flops 538443776 | bytes 4459008 | tf_op jit(solution)/shard_map/while/body/eval_jaxpr/dot_general | solution.py:53
  126.3 3.1 %fusion.47 = f32[2048,256]{1,0:T(8,128)S(1)} fusion(f32[2048,256]{1,0:T(8,128)} %get-tuple-element.204, s32[512]{0:T(512)S(1)} %bitcast.57, pred[]{:T(512)S(6)} %compare.3, bf16[8,512,256]{2,1,0:T(8,128)(2,1)} %get-tuple-element.213, s32[]{:T(128)} %get-tuple-element.203), kind=kOutput, calls=%fused_computation.12.clone.1 | convolution fusion | flops 538968064 | bytes 4459009 | tf_op jit(solution)/shard_map/while/body/eval_jaxpr/dot_general | solution.py:50
  129.4 3.7 %fusion.48 = f32[2048,256]{1,0:T(8,128)} fusion(f32[2048,256]{1,0:T(8,128)S(1)} %fusion.47, s32[512]{0:T(512)S(1)} %bitcast.58, bf16[8,512,256]{2,1,0:T(8,128)(2,1)} %get-tuple-element.214, s32[]{:T(128)} %get-tuple-element.203), kind=kOutput, calls=%fused_computation.13.clone.1 | convolution fusion | flops 538443776 | bytes 4459008 | tf_op jit(solution)/shard_map/while/body/eval_jaxpr/dot_general | solution.py:53
  133.1 3.1 %fusion.47 = f32[2048,256]{1,0:T(8,128)S(1)} fusion(f32[2048,256]{1,0:T(8,128)} %get-tuple-element.204, s32[512]{0:T(512)S(1)} %bitcast.57, pred[]{:T(512)S(6)} %compare.3, bf16[8,512,256]{2,1,0:T(8,128)(2,1)} %get-tuple-element.213, s32[]{:T(128)} %get-tuple-element.203), kind=kOutput, calls=%fused_computation.12.clone.1 | convolution fusion | flops 538968064 | bytes 4459009 | tf_op jit(solution)/shard_map/while/body/eval_jaxpr/dot_general | solution.py:50
  136.3 3.7 %fusion.48 = f32[2048,256]{1,0:T(8,128)} fusion(f32[2048,256]{1,0:T(8,128)S(1)} %fusion.47, s32[512]{0:T(512)S(1)} %bitcast.58, bf16[8,512,256]{2,1,0:T(8,128)(2,1)} %get-tuple-element.214, s32[]{:T(128)} %get-tuple-element.203), kind=kOutput, calls=%fused_computation.13.clone.1 | convolution fusion | flops 538443776 | bytes 4459008 | tf_op jit(solution)/shard_map/while/body/eval_jaxpr/dot_general | solution.py:53
  140.0 3.1 %fusion.47 = f32[2048,256]{1,0:T(8,128)S(1)} fusion(f32[2048,256]{1,0:T(8,128)} %get-tuple-element.204, s32[512]{0:T(512)S(1)} %bitcast.57, pred[]{:T(512)S(6)} %compare.3, bf16[8,512,256]{2,1,0:T(8,128)(2,1)} %get-tuple-element.213, s32[]{:T(128)} %get-tuple-element.203), kind=kOutput, calls=%fused_computation.12.clone.1 | convolution fusion | flops 538968064 | bytes 4459009 | tf_op jit(solution)/shard_map/while/body/eval_jaxpr/dot_general | solution.py:50
  143.1 3.7 %fusion.48 = f32[2048,256]{1,0:T(8,128)} fusion(f32[2048,256]{1,0:T(8,128)S(1)} %fusion.47, s32[512]{0:T(512)S(1)} %bitcast.58, bf16[8,512,256]{2,1,0:T(8,128)(2,1)} %get-tuple-element.214, s32[]{:T(128)} %get-tuple-element.203), kind=kOutput, calls=%fused_computation.13.clone.1 | convolution fusion | flops 538443776 | bytes 4459008 | tf_op jit(solution)/shard_map/while/body/eval_jaxpr/dot_general | solution.py:53
  146.8 3.1 %fusion.47 = f32[2048,256]{1,0:T(8,128)S(1)} fusion(f32[2048,256]{1,0:T(8,128)} %get-tuple-element.204, s32[512]{0:T(512)S(1)} %bitcast.57, pred[]{:T(512)S(6)} %compare.3, bf16[8,512,256]{2,1,0:T(8,128)(2,1)} %get-tuple-element.213, s32[]{:T(128)} %get-tuple-element.203), kind=kOutput, calls=%fused_computation.12.clone.1 | convolution fusion | flops 538968064 | bytes 4459009 | tf_op jit(solution)/shard_map/while/body/eval_jaxpr/dot_general | solution.py:50
  149.9 3.7 %fusion.48 = f32[2048,256]{1,0:T(8,128)} fusion(f32[2048,256]{1,0:T(8,128)S(1)} %fusion.47, s32[512]{0:T(512)S(1)} %bitcast.58, bf16[8,512,256]{2,1,0:T(8,128)(2,1)} %get-tuple-element.214, s32[]{:T(128)} %get-tuple-element.203), kind=kOutput, calls=%fused_computation.13.clone.1 | convolution fusion | flops 538443776 | bytes 4459008 | tf_op jit(solution)/shard_map/while/body/eval_jaxpr/dot_general | solution.py:53
  153.7 3.1 %fusion.47 = f32[2048,256]{1,0:T(8,128)S(1)} fusion(f32[2048,256]{1,0:T(8,128)} %get-tuple-element.204, s32[512]{0:T(512)S(1)} %bitcast.57, pred[]{:T(512)S(6)} %compare.3, bf16[8,512,256]{2,1,0:T(8,128)(2,1)} %get-tuple-element.213, s32[]{:T(128)} %get-tuple-element.203), kind=kOutput, calls=%fused_computation.12.clone.1 | convolution fusion | flops 538968064 | bytes 4459009 | tf_op jit(solution)/shard_map/while/body/eval_jaxpr/dot_general | solution.py:50
  156.8 3.7 %fusion.48 = f32[2048,256]{1,0:T(8,128)} fusion(f32[2048,256]{1,0:T(8,128)S(1)} %fusion.47, s32[512]{0:T(512)S(1)} %bitcast.58, bf16[8,512,256]{2,1,0:T(8,128)(2,1)} %get-tuple-element.214, s32[]{:T(128)} %get-tuple-element.203), kind=kOutput, calls=%fused_computation.13.clone.1 | convolution fusion | flops 538443776 | bytes 4459008 | tf_op jit(solution)/shard_map/while/body/eval_jaxpr/dot_general | solution.py:53
  160.5 36.2 %all-reduce.3.cloned.1.call-done = (f32[256,1024]{1,0:T(8,128)}, f32[768,256]{0,1:T(8,128)}) async-done(((f32[256,1024]{1,0:T(8,128)}, f32[768,256]{0,1:T(8,128)}), (f32[256,1024]{1,0:T(8,128)}, f32[768,256]{0,1:T(8,128)})) %all-reduce.3.cloned.1.call-update) | async-done | bytes 1835024 | tf_op jit(solution)/shard_map/psum | solution.py:101
  196.7 1.0 constant_dynamic-slice_fusion.2
  197.8 0.7 copy.19
  198.5 1.4 dynamic-slice_bitcast_fusion
  (30 shorter events, 0.2 us)
Async XLA Ops:
  8.0 72.7 %copy-start = (bf16[1,4608,256]{2,1,0:T(8,128)(2,1)S(1)}, bf16[1,4608,256]{2,1,0:T(8,128)(2,1)}, u32[]{:S(2)}) copy-start(bf16[1,4608,256]{2,1,0:T(8,128)(2,1)} %param.13) | copy-start | bytes 7077892
  9.5 17.0 %all-to-all-start.2 = ((s32[32,1,1]{2,1,0:T(1,128)}), s32[32,1,1]{2,1,0:T(1,128)S(1)}, u32[]{:S(2)}, u32[]{:S(2)}) async-start(s32[32,1,1]{2,1,0:T(1,128)} %copy.16), calls=%async_computation.2 | async-start | bytes 32768 | tf_op jit(solution)/shard_map/all_to_all | solution.py:84
  26.5 40.0 %all-to-all-start = ((s32[32,1,128]{2,1,0:T(1,128)}), s32[32,1,128]{2,1,0:T(1,128)S(1)}, u32[]{:S(2)}, u32[]{:S(2)}) async-start(s32[32,1,128]{2,1,0:T(1,128)} %bitcast), calls=%async_computation | async-start | bytes 32768 | tf_op jit(solution)/shard_map/all_to_all | solution.py:83
  66.5 36.4 %all-to-all-start.1 = ((bf16[32,128,256]{2,1,0:T(8,128)(2,1)}), bf16[32,128,256]{2,1,0:T(8,128)(2,1)}, u32[]{:S(2)}, u32[]{:S(2)}) async-start(bf16[32,128,256]{2,1,0:T(8,128)(2,1)} %bitcast.56), calls=%async_computation.1 | async-start | bytes 4194304 | tf_op jit(solution)/shard_map/all_to_all | solution.py:82
  74.0 122.7 %all-reduce.3.cloned.1.call-start = ((), (), s32[]{:S(2)}) async-start(), calls=%async_computation.5 | async-start | bytes 3670016 | tf_op jit(solution)/shard_map/psum | solution.py:101
  88.1 111.8 %reduce-scatter.2.cloned.1.call-start = ((), (), s32[]{:S(2)}) async-start(), calls=%async_computation.4 | async-start | bytes 2621440 | tf_op jit(solution)/shard_map/reduce_scatter | solution.py:90
Sparse Core Ops, SparseCore 0:
  88.2 108.4 all-reduce.2
Sparse Core Ops, SparseCore 1:
  160.6 26.8 reduce-scatter.1
where the time goes:
time: 209 us; the launch traced here: 207 us
  matrix products  108 us (52%)
  waiting for transfers between devices  48.6 us (23%)
  starting transfers between devices  23.6 us (11%)
  between operations  15.6 us (7%)
  local copies, waits for them, and re-layouts  6.21 us (3%)
  other arithmetic  5.02 us (2%)
    psum x1, waiting for transfers between devices, on_device(): rel_total, self_total = lax.psum((rel_term, self_term), 'nodes')  36.2 us
    dot_general x8, matrix products, one_block(): jnp.dot(onehot, table_bf, preferred_element_type=jnp.float32)  32.6 us
    dot_general x8, matrix products, add_block(): lax.dot_general(onehot, low_rows, contract, preferred_element_type=jnp.fl...  29.6 us
    dot_general x8, matrix products, add_block(): lax.dot_general(onehot, high_rows, contract, preferred_element_type=jnp.f...  24.2 us
    all_to_all x1, waiting for transfers between devices, on_device(): lax.all_to_all(messages, 'nodes', split_axis=0, concat_axis=0, tiled=True)  12.4 us
    all_to_all x1, starting transfers between devices, on_device(): lax.all_to_all(counts, 'nodes', split_axis=0, concat_axis=0, tiled=True)  8.42 us
    dot_general x1, matrix products, on_device(): lax.dot_general(grad_out, weight, (((1,), (1,)), ((), ())), preferred_ele...  7.79 us
    all_to_all x1, starting transfers between devices, on_device(): lax.all_to_all(messages, 'nodes', split_axis=0, concat_axis=0, tiled=True)  7.51 us
  transfers between devices with their start and end apart: 5, of which 2 were waited for; matrix products, arithmetic and copies ran while one was open for 57% of the time, Pallas kernels for 0%

commit v1 on v0

v1 whole, which is shorter than its diff:
```python
import jax
import jax.numpy as jnp
from jax import lax
from jax.experimental import pallas as pl
from jax.experimental.pallas import tpu as pltpu
from jax.sharding import PartitionSpec as P

MESH = pl.DeviceIdType.MESH
F32 = jnp.float32
BF16 = jnp.bfloat16
DOTS = dict(preferred_element_type=F32)

NODES, REL = 32, 4
YN, ZN, CN = 4, 4, 2
PAPERS, OUT_W, AUTH_W, PAPER_W = 4608, 1024, 256, 768
SLOTS, GROUP, OWN = 128, 2048, 512
CHUNK = 768
CHUNKS = PAPERS // CHUNK
PIECE = 112
PER_SCAT = 4
SCAT_ROWS = 1024
WHOLE = 24
LATE = NODES - WHOLE
HALF = AUTH_W // 2
PART = OWN // 2


def chunk(k):
    return pl.ds(pl.multiple_of(k * CHUNK, CHUNK), CHUNK)


def block(t):
    if isinstance(t, int):
        return pl.ds(t * SLOTS, SLOTS)
    return pl.ds(pl.multiple_of(t * SLOTS, SLOTS), SLOTS)


ROW, COLUMN = 0, 1
GROUPS = [(ROW, 2, 0), (ROW, 2, 1), (COLUMN, 2), (ROW, 0, 0), (ROW, 0, 1), (COLUMN, 0), (COLUMN, 1), (COLUMN, 3)]


def in_group(group, j):
    if group[0] == ROW:
        return group[1], j, group[2]
    return 1 + 2 * (j // 2), group[1], j % 2


SLOT_OFFSETS = [in_group(group, j) for group in GROUPS for j in range(4)]
HERE = SLOT_OFFSETS.index((0, 0, 0))
OTHERS = [t for t in range(NODES) if t != HERE]
RELAYED = [t for t in OTHERS if 2 in SLOT_OFFSETS[t][:2]]
DIRECT = [t for t in OTHERS if t < WHOLE and t not in RELAYED]


def first_hop(t):
    dy, dz, dc = SLOT_OFFSETS[t]
    step = 1 + 2 * dc
    return step * (dy == 2), step * (dz == 2), 0


def second_hop(t):
    dy, dz, dc = SLOT_OFFSETS[t]
    hy, hz, _ = first_hop(t)
    return (dy - hy) % YN, (dz - hz) % ZN, dc


class Place:
    def __init__(self):
        me = lax.axis_index("nodes")
        self.me = me
        self.y = lax.div(me, ZN * CN)
        self.z = lax.rem(lax.div(me, CN), ZN)
        self.c = lax.rem(me, CN)
        sign = 1 + 2 * self.c
        self.ys = [lax.rem(self.y + sign * k, YN) * (ZN * CN) for k in range(YN)]
        self.zs = [lax.rem(self.z + sign * k, ZN) * CN for k in range(ZN)]
        self.cs = [self.c, 1 - self.c]
        self.sign = sign

    def node(self, dy, dz, dc):
        return self.ys[dy] + self.zs[dz] + self.cs[dc]

    def peer(self, t):
        return self.node(*SLOT_OFFSETS[t])

    def peer_in(self, k, j):
        group = GROUPS[k]
        if group[0] == ROW:
            return self.ys[group[1]] + lax.rem(self.z + self.sign * j, ZN) * CN + self.cs[group[2]]
        y = lax.rem(self.y + self.sign * (1 + 2 * lax.div(j, 2)), YN)
        return y * (ZN * CN) + self.zs[group[1]] + lax.rem(self.c + lax.rem(j, 2), CN)


def each(slots, body):
    for t in slots:
        body(t)


def loop(lo, hi, body):
    def step(t, _):
        body(t)
        return 0

    lax.fori_loop(lo, hi, step, 0)


def kernel(
    papers, counts, authors, w_hbm, go_hbm, pf_hbm, sa_hbm,
    ga, gr, gs,
    w, wt, g, feat, agg, table, rows, send, relay, recv, late_send, late_recv, auth, acc,
    racc, sacc, wg, csend, crecv, yfar_send, yfar_recv, ynear_send, ynear_recv, own_sum, zsend, zrecv,
    far_send, far_recv, near_send, near_recv,
    wsem, gsem, fsem, asem, au_s, au_r, ms_s, ms_r, rl_s, rl_r, lt_s, lt_r,
    c_s, c_r, yf_s, yf_r, yn_s, yn_r, z_s, z_r, far_s, far_r, near_s, near_r,
):
    at = Place()
    q = lax.axis_index("rel")
    me, y, z, c, node = at.me, at.y, at.z, at.c, at.node

    def g_copy(k):
        return pltpu.make_async_copy(go_hbm.at[chunk(k)], g.at[chunk(k)], gsem.at[k])

    def f_copy(k):
        return pltpu.make_async_copy(pf_hbm.at[chunk(k)], feat.at[chunk(k)], fsem.at[k])

    def a_copy(k):
        return pltpu.make_async_copy(sa_hbm.at[chunk(k)], agg.at[chunk(k)], asem.at[k])

    def load_rest(k):
        a_copy(k).start()
        f_copy(k).start()

    w_copy = pltpu.make_async_copy(w_hbm, w, wsem)
    w_copy.start()
    loop(0, CHUNKS, lambda k: g_copy(k).start())

    barrier = pltpu.get_barrier_semaphore()

    def greet(t):
        pl.semaphore_signal(barrier, inc=1, device_id={"nodes": at.peer(t)}, device_id_type=MESH)

    each(OTHERS, greet)
    for d in (1, REL - 1):
        pl.semaphore_signal(
            barrier, inc=1, device_id={"rel": lax.rem(q + d, REL)}, device_id_type=MESH
        )

    w_copy.wait()
    wt[...] = w[...].astype(F32).T.astype(BF16)

    def back_step(k):
        g_copy(k).wait()
        part = CHUNK // 2
        for m in range(2):
            lo = k * CHUNK + m * part
            back = jnp.dot(g[pl.ds(pl.multiple_of(lo, part), part), :], wt[...], **DOTS)
            for h in range(2):
                table[pl.ds(2 * lo + h, part, stride=2), :] = back[:, h * HALF:h * HALF + HALF]

    loop(0, CHUNKS, back_step)
    loop(0, CHUNKS, load_rest)
    pl.semaphore_wait(barrier, NODES - 1 + 2)

    def remote(src, dst, sems, i, to):
        return pltpu.make_async_remote_copy(
            src_ref=src, dst_ref=dst, send_sem=sems[0].at[i], recv_sem=sems[1].at[i],
            device_id={"nodes": to}, device_id_type=MESH,
        )

    def auth_copy(t):
        return remote(authors.at[at.peer(t)], auth.at[t], (au_s, au_r), t, at.peer(t))

    def relay_copy(t):
        i = RELAYED.index(t)
        return remote(send.at[block(t)], relay.at[block(i)], (rl_s, rl_r), i, node(*first_hop(t)))

    def msg_copy(t):
        if t in RELAYED:
            source, to = relay.at[block(RELAYED.index(t))], node(*second_hop(t))
        else:
            source, to = send.at[block(t)], at.peer(t)
        return remote(source, recv.at[block(t)], (ms_s, ms_r), t, to)

    def late_copy(h, i):
        return remote(
            late_send.at[h, block(i)], late_recv.at[h, block(i)],
            (lt_s, lt_r), h * LATE + i, at.peer(WHOLE + i),
        )

    def gather(b):
        for u in range(SLOTS):
            p = papers[b, u] * 2
            rows[2 * u:2 * u + 2, :] = table[pl.ds(p, 2), :]
        live = counts[b]
        scale = lax.rsqrt(jnp.full((1, HALF), live, jnp.int32).astype(F32))
        slot = lax.broadcasted_iota(jnp.int32, (SLOTS, HALF), 0)
        return [
            jnp.where(slot < live, rows[pl.ds(h, SLOTS, stride=2), :] * scale, 0.0).astype(BF16)
            for h in range(2)
        ]

    for k in range(WHOLE // 4):

        def whole_step(j):
            left, right = gather(at.peer_in(k, j))
            send[block(k * 4 + j), :HALF] = left
            send[block(k * 4 + j), HALF:] = right

        loop(0, 4, whole_step)
        for t in range(k * 4, k * 4 + 4):
            if t in RELAYED:
                relay_copy(t).start()
            elif t != HERE:
                msg_copy(t).start()
    for k in range(LATE // 4):

        def late_step(j):
            left, right = gather(at.peer_in(WHOLE // 4 + k, j))
            late_send[0, block(k * 4 + j), :] = left
            late_send[1, block(k * 4 + j), :] = right

        loop(0, 4, late_step)
    each(OTHERS, lambda t: auth_copy(t).start())
    auth[HERE] = authors[me]
    recv[block(HERE), :] = send[block(HERE), :]

    racc[...] = jnp.zeros_like(racc)
    sacc[...] = jnp.zeros_like(sacc)
    cols = pl.ds(pl.multiple_of(q * AUTH_W, AUTH_W), AUTH_W)
    over0 = (((0,), (0,)), ((), ()))

    def grads_step(k):
        a_copy(k).wait()
        f_copy(k).wait()
        racc[...] += lax.dot_general(agg[chunk(k), :], g[chunk(k), :], over0, **DOTS)
        sacc[...] += lax.dot_general(g[chunk(k), cols], feat[chunk(k), :], over0, **DOTS)

    def forward(t):
        relay_copy(t).wait_recv()
        msg_copy(t).start()

    loop(0, 2, grads_step)
    each(RELAYED, forward)
    loop(2, CHUNKS, grads_step)

    sacc_t = sacc[...].T
    for n in range(NODES):
        co, yz = n % CN, n // CN
        for k in range(8):
            wg[co, yz, 8 * k:8 * k + 8, :] = racc[8 * n:8 * n + 8, 128 * k:128 * k + 128]
        for i in range(3):
            for h in range(2):
                r0 = 64 + (2 * i + h) * 8
                wg[co, yz, r0:r0 + 8, :] = sacc_t[24 * n + 8 * i:24 * n + 8 * i + 8, 128 * h:128 * h + 128]

    core_copy = pltpu.make_async_remote_copy(
        src_ref=csend, dst_ref=crecv, send_sem=c_s, recv_sem=c_r,
        device_id={"nodes": node(0, 0, 1)}, device_id_type=MESH,
    )

    def core_round(i):
        csend[i] = wg[1 - c, i].astype(BF16)

    loop(0, YN * ZN, core_round)
    core_copy.start()
    for h in range(2):
        each(range(LATE), lambda i: late_copy(h, i).start())

    acc[...] = jnp.zeros_like(acc)
    each(OTHERS, lambda t: auth_copy(t).wait_recv())

    def add_rows(first_slot, msg, cols):
        targets = [auth[first_slot + u] for u in range(PER_SCAT)]

        def some(m):
            span = pl.ds(pl.multiple_of(m * SCAT_ROWS, SCAT_ROWS), SCAT_ROWS)
            ids = lax.broadcasted_iota(jnp.int32, (SCAT_ROWS, SLOTS), 0) + m * SCAT_ROWS
            onehot = jnp.concatenate(
                [jnp.where(ids == a, 1.0, 0.0).astype(BF16) for a in targets], axis=1
            )
            acc[span, cols] += jnp.dot(onehot, msg, **DOTS)

        loop(0, GROUP // SCAT_ROWS, some)

    def group(s):
        width = PER_SCAT * SLOTS
        return pl.ds(pl.multiple_of(s * width, width), width)

    def scatter(s):
        for u in range(PER_SCAT):
            if s * PER_SCAT + u != HERE:
                msg_copy(s * PER_SCAT + u).wait_recv()
        add_rows(s * PER_SCAT, recv[group(s), :], slice(None))

    def scatter_late(h, s):
        for u in range(PER_SCAT):
            late_copy(h, s * PER_SCAT + u).wait_recv()
        add_rows(WHOLE + s * PER_SCAT, late_recv[h, group(s), :], slice(h * HALF, h * HALF + HALF))

    def y_to(d):
        return lax.div(at.ys[1 + 2 * d], ZN * CN)

    def pair(to, p):
        return to * ZN + 2 * p

    def yfar_copy(d):
        return remote(yfar_send.at[d], yfar_recv.at[d], (yf_s, yf_r), d, node(1 + 2 * d, 0, 0))

    def ynear_copy(d, p):
        return remote(
            ynear_send.at[d, p], ynear_recv.at[d, p], (yn_s, yn_r), 2 * d + p, node(1 + 2 * d, 0, 0)
        )

    def z_copy(d):
        to = lax.div(at.zs[d], CN)
        return remote(zsend.at[to], zrecv.at[d - 1], (z_s, z_r), d - 1, node(0, d, 0))

    def core_sum(i):
        wg[c, i] = wg[c, i] + crecv[i].astype(F32)

    def y_first():
        core_copy.wait_recv()
        loop(0, YN * ZN, core_sum)
        for d in range(2):
            for i in range(2):
                yfar_send[d, i] = wg[c, pair(lax.rem(y + 2, YN), d) + i].astype(BF16)
            yfar_copy(d).start()
        for d in range(2):
            for i in range(2):
                ynear_send[d, 1 - d, i] = wg[c, pair(y_to(d), 1 - d) + i].astype(BF16)
            ynear_copy(d, 1 - d).start()

    def y_second():
        for d in range(2):
            yfar_copy(d).wait_recv()
            for i in range(2):
                total = wg[c, pair(y_to(d), d) + i] + yfar_recv[d, i].astype(F32)
                ynear_send[d, d, i] = total.astype(BF16)
            ynear_copy(d, d).start()

    def z_first():
        for p in range(2):
            for d in range(2):
                ynear_copy(d, p).wait_recv()
            for i in range(2):
                total = (
                    wg[c, pair(y, p) + i]
                    + ynear_recv[0, p, i].astype(F32) + ynear_recv[1, p, i].astype(F32)
                )
                own_sum[2 * p + i] = total
                zsend[2 * p + i] = total.astype(BF16)
        for d in range(1, ZN):
            z_copy(d).start()

    def z_last():
        for d in range(1, ZN):
            z_copy(d).wait_recv()
        total = own_sum[z]
        for d in range(ZN - 1):
            total = total + zrecv[d].astype(F32)
        for k in range(8):
            gr[:, 128 * k:128 * k + 128] = total[8 * k:8 * k + 8, :]
        for i in range(3):
            for h in range(2):
                r0 = 64 + (2 * i + h) * 8
                gs[8 * i:8 * i + 8, 128 * h:128 * h + 128] = total[r0:r0 + 8, :]

    def towards(d):
        return lax.rem(q + (1, REL - 1)[d], REL)

    def rows_of(owner, p):
        return pl.ds(pl.multiple_of(owner * OWN + p * PART, PART), PART)

    def far_copy(h, d):
        return pltpu.make_async_remote_copy(
            src_ref=far_send.at[h, d], dst_ref=far_recv.at[h, d],
            send_sem=far_s.at[h, d], recv_sem=far_r.at[h, d],
            device_id={"rel": towards(d)}, device_id_type=MESH,
        )

    def near_copy(h, d, p):
        return pltpu.make_async_remote_copy(
            src_ref=near_send.at[h, d, p], dst_ref=near_recv.at[h, d, p],
            send_sem=near_s.at[h, d, p], recv_sem=near_r.at[h, d, p],
            device_id={"rel": towards(d)}, device_id_type=MESH,
        )

    def half(h):
        return slice(h * HALF, h * HALF + HALF)

    def rel_first(h):
        for d in range(2):
            far_send[h, d] = acc[rows_of(lax.rem(q + 2, REL), d), half(h)].astype(BF16)
            far_copy(h, d).start()
        for d in range(2):
            near_send[h, d, 1 - d] = acc[rows_of(towards(d), 1 - d), half(h)].astype(BF16)
            near_copy(h, d, 1 - d).start()

    def rel_second(h):
        for d in range(2):
            far_copy(h, d).wait_recv()
            mine = acc[rows_of(towards(d), d), half(h)]
            near_send[h, d, d] = (mine + far_recv[h, d].astype(F32)).astype(BF16)
            near_copy(h, d, d).start()

    def rel_last(h):
        for p in range(2):
            for d in range(2):
                near_copy(h, d, p).wait_recv()
            ga[p * PART:p * PART + PART, half(h)] = (
                acc[rows_of(q, p), half(h)]
                + near_recv[h, 0, p].astype(F32) + near_recv[h, 1, p].astype(F32)
            )

    scatter(3)
    scatter(5)
    scatter(4)
    y_first()
    scatter(0)
    scatter(1)
    y_second()
    scatter(2)
    scatter_late(0, 0)
    scatter_late(0, 1)
    rel_first(0)
    z_first()
    scatter_late(1, 0)
    rel_second(0)
    scatter_late(1, 1)
    rel_first(1)
    z_last()
    rel_last(0)
    rel_second(1)
    rel_last(1)

    core_copy.wait_send()
    each(OTHERS, lambda t: auth_copy(t).wait_send())
    each(RELAYED, lambda t: relay_copy(t).wait_send())
    each(RELAYED + DIRECT, lambda t: msg_copy(t).wait_send())
    for h in range(2):
        each(range(LATE), lambda i: late_copy(h, i).wait_send())
        for d in range(2):
            far_copy(h, d).wait_send()
            for p in range(2):
                near_copy(h, d, p).wait_send()
    for d in range(2):
        yfar_copy(d).wait_send()
        for p in range(2):
            ynear_copy(d, p).wait_send()
    for d in range(1, ZN):
        z_copy(d).wait_send()


def hand_over(a, b, c, ao, bo, co):
    ao[...] = a[...]
    bo[...] = b[...]
    co[...] = c[...]


def on_device(grad_out, paper_feat, saved_agg, rel_weight, slot_paper, slot_author, block_count):
    vmem = pl.BlockSpec(memory_space=pltpu.VMEM)
    smem = pl.BlockSpec(memory_space=pltpu.SMEM)
    hbm = pl.BlockSpec(memory_space=pl.ANY)
    dma = pltpu.SemaphoreType.DMA
    limit = 56 * 1024 * 1024
    whole = (WHOLE * SLOTS, AUTH_W)
    late = (2, LATE * SLOTS, HALF)
    ga, gr, gs = pl.pallas_call(
        kernel,
        out_shape=(
            jax.ShapeDtypeStruct((OWN, AUTH_W), F32),
            jax.ShapeDtypeStruct((8, OUT_W), F32),
            jax.ShapeDtypeStruct((24, AUTH_W), F32),
        ),
        in_specs=[smem, smem, vmem, hbm, hbm, hbm, hbm],
        out_specs=(vmem, vmem, vmem),
        scratch_shapes=[
            pltpu.VMEM((AUTH_W, OUT_W), BF16),
            pltpu.VMEM((OUT_W, AUTH_W), BF16),
            pltpu.VMEM((PAPERS, OUT_W), BF16),
            pltpu.VMEM((PAPERS, PAPER_W), BF16),
            pltpu.VMEM((PAPERS, AUTH_W), BF16),
            pltpu.VMEM((2 * PAPERS, HALF), F32),
            pltpu.VMEM((2 * SLOTS, HALF), F32),
            pltpu.VMEM(whole, BF16),
            pltpu.VMEM((len(RELAYED) * SLOTS, AUTH_W), BF16),
            pltpu.VMEM(whole, BF16),
            pltpu.VMEM(late, BF16),
            pltpu.VMEM(late, BF16),
            pltpu.VMEM((NODES, 1, SLOTS), jnp.int32),
            pltpu.VMEM((GROUP, AUTH_W), F32),
            pltpu.VMEM((AUTH_W, OUT_W), F32),
            pltpu.VMEM((AUTH_W, PAPER_W), F32),
            pltpu.VMEM((CN, YN * ZN, PIECE, 128), F32),
            pltpu.VMEM((YN * ZN, PIECE, 128), BF16),
            pltpu.VMEM((YN * ZN, PIECE, 128), BF16),
            pltpu.VMEM((2, 2, PIECE, 128), BF16),
            pltpu.VMEM((2, 2, PIECE, 128), BF16),
            pltpu.VMEM((2, 2, 2, PIECE, 128), BF16),
            pltpu.VMEM((2, 2, 2, PIECE, 128), BF16),
            pltpu.VMEM((ZN, PIECE, 128), F32),
            pltpu.VMEM((ZN, PIECE, 128), BF16),
            pltpu.VMEM((ZN - 1, PIECE, 128), BF16),
            pltpu.VMEM((2, 2, PART, HALF), BF16),
            pltpu.VMEM((2, 2, PART, HALF), BF16),
            pltpu.VMEM((2, 2, 2, PART, HALF), BF16),
            pltpu.VMEM((2, 2, 2, PART, HALF), BF16),
            dma, dma((CHUNKS,)), dma((CHUNKS,)), dma((CHUNKS,)),
            dma((NODES,)), dma((NODES,)), dma((WHOLE,)), dma((WHOLE,)),
            dma((len(RELAYED),)), dma((len(RELAYED),)), dma((2 * LATE,)), dma((2 * LATE,)),
            dma, dma, dma((2,)), dma((2,)), dma((4,)), dma((4,)), dma((3,)), dma((3,)),
            dma((2, 2)), dma((2, 2)), dma((2, 2, 2)), dma((2, 2, 2)),
        ],
        compiler_params=pltpu.CompilerParams(
            collective_id=0, has_side_effects=True, vmem_limit_bytes=limit
        ),
    )(
        slot_paper[0, 0], block_count[0, 0],
        slot_author[0, 0][:, None, :], rel_weight[0], grad_out, paper_feat, saved_agg[0],
    )
    ga, gr, gs = pl.pallas_call(
        hand_over,
        out_shape=tuple(jax.ShapeDtypeStruct(v.shape, F32) for v in (ga, gr, gs)),
        in_specs=[vmem] * 3,
        out_specs=(vmem,) * 3,
    )(ga, gr, gs)
    return ga, gr[None], gs


def solution(mesh):
    return jax.shard_map(
        on_device,
        mesh=mesh,
        in_specs=(
            P("nodes", None),
            P("nodes", None),
            P("rel", "nodes", None),
            P("rel", None, None),
            P("nodes", "rel", None, None),
            P("nodes", "rel", None, None),
            P("nodes", "rel", None),
        ),
        out_specs=(P(("nodes", "rel"), None), P("rel", "nodes", None), P("nodes", "rel")),
        check_vma=False,
    )
```

time: 209 us -> 65.3 us (0.31)
  matrix products: 108 us -> 0 us
  Pallas kernels: 0 us -> 64.5 us
  waiting for transfers between devices: 48.6 us -> 0 us
  starting transfers between devices: 23.6 us -> 0 us
  between operations: 15.6 us -> 0.64 us
  local copies, waits for them, and re-layouts: 6.21 us -> 0 us
  other arithmetic: 5.02 us -> 0 us
    dot_general x27 -> x0, matrix products: 108 us -> none  [the longest x8 32.6 us: one_block(): jnp.dot(onehot, table_bf, preferred_element_type=jnp.float32)]
    pallas_call x0 -> x2, Pallas kernels: none -> 64.5 us  [the longest x1 62.6 us: on_device(): pl.pallas_call(kernel, out_shape=(jax.ShapeDtypeStruct((OWN, AUTH_W), F32...]
    psum x1 -> x0, waiting for transfers between devices: 36.2 us -> none  [on_device(): rel_total, self_total = lax.psum((rel_term, self_term), 'nodes')]
    all_to_all x3 -> x0, starting transfers between devices: 23.3 us -> none  [the longest x1 8.42 us: on_device(): lax.all_to_all(counts, 'nodes', split_axis=0, concat_axis=0, tiled=True)]
    all_to_all x3 -> x0, waiting for transfers between devices: 12.4 us -> none  [the longest x1 12.4 us: on_device(): lax.all_to_all(messages, 'nodes', split_axis=0, concat_axis=0, tiled=True)]
    convert_element_type x1 -> x0, other arithmetic: 3.6 us -> none  [rows_sum(): low_part = (scaled - high_part.astype(jnp.float32)).astype(jnp.bfloat16)]
  transfers between devices with their start and end apart: 5 -> 0, of which waited for: 2 -> 0; matrix products, arithmetic and copies ran while one was open for 57% -> 0% of each run, Pallas kernels for 0% -> 0%
where the time goes in v1:
time: 65.3 us; the launch traced here: 65.1 us
  Pallas kernels  64.5 us (99%)
    pallas_call x1, Pallas kernels, on_device(): pl.pallas_call(kernel, out_shape=(jax.ShapeDtypeStruct((OWN, AUTH_W), F32...  62.6 us
    pallas_call x1, Pallas kernels, on_device(): pl.pallas_call(hand_over, out_shape=tuple((jax.ShapeDtypeStruct(v.shape,...  1.9 us

profile of v1, /device:TPU:0, one launch (start us, length us, event | category | flops | bytes accessed | tf_op | source)
XLA Modules:
  0.0 65.1 jit_solution(10940432869360987374)
XLA Ops:
  0.6 62.6 %shard_map.94 = (f32[512,256]{1,0:T(8,128)}, f32[8,1024]{1,0:T(8,128)}, f32[24,256]{1,0:T(8,128)}) custom-call(s32[32,128]{1,0:T(8,128)} %bitcast.8, s32[32]{0:T(128)} %bitcast.10, s32[32,1,128]{2,1,0:T(1,128)} %bitcast.9, bf16[256,1024]{1,0:T(8,128)(2,1)} %bitcast.7, bf16[4608,1024]{1,0:T(8,128)(2,1)} %go_hbm.1, bf16[4608,768]{1,0:T(8,128)(2,1)} %pf_hbm.1, ...), custom_call_target="tpu_custom_call" | custom-call | tf_op jit(solution)/shard_map/pallas_call | solution.py:468
  63.2 1.9 %shard_map.95 = (f32[512,256]{1,0:T(8,128)}, f32[8,1024]{1,0:T(8,128)}, f32[24,256]{1,0:T(8,128)}) custom-call(f32[512,256]{1,0:T(8,128)} %get-tuple-element.9.a, f32[8,1024]{1,0:T(8,128)} %get-tuple-element.10.b, f32[24,256]{1,0:T(8,128)} %get-tuple-element.11.c), custom_call_target="tpu_custom_call" | custom-call | tf_op jit(solution)/shard_map/pallas_call | solution.py:521

commit v2 on v1

--- a/solution.py
+++ b/solution.py
@@ -11,7 +11,7 @@
 DOTS = dict(preferred_element_type=F32)
 
 NODES, REL = 32, 4
-YN, ZN, CN = 4, 4, 2
+SIDE, CN = 4, 2
 PAPERS, OUT_W, AUTH_W, PAPER_W = 4608, 1024, 256, 768
 SLOTS, GROUP, OWN = 128, 2048, 512
 CHUNK = 768
@@ -36,7 +36,7 @@
 
 
 ROW, COLUMN = 0, 1
-GROUPS = [(ROW, 2, 0), (ROW, 2, 1), (COLUMN, 2), (ROW, 0, 0), (ROW, 0, 1), (COLUMN, 0), (COLUMN, 1), (COLUMN, 3)]
+GROUPS = [(ROW, 2, 0), (COLUMN, 2), (ROW, 2, 1), (ROW, 0, 0), (COLUMN, 0), (ROW, 0, 1), (COLUMN, 1), (COLUMN, 3)]
 
 
 def in_group(group, j):
@@ -53,32 +53,37 @@
 
 
 def first_hop(t):
-    dy, dz, dc = SLOT_OFFSETS[t]
-    step = 1 + 2 * dc
-    return step * (dy == 2), step * (dz == 2), 0
+    da, db, dc = SLOT_OFFSETS[t]
+    ha = (1 if db < 2 else 3) if da == 2 else 0
+    hb = (1 if da in (1, 2) else 3) if db == 2 else 0
+    return ha, hb, 0
 
 
 def second_hop(t):
-    dy, dz, dc = SLOT_OFFSETS[t]
-    hy, hz, _ = first_hop(t)
-    return (dy - hy) % YN, (dz - hz) % ZN, dc
+    da, db, dc = SLOT_OFFSETS[t]
+    ha, hb, _ = first_hop(t)
+    return (da - ha) % SIDE, (db - hb) % SIDE, dc
 
 
 class Place:
     def __init__(self):
         me = lax.axis_index("nodes")
-        self.me = me
-        self.y = lax.div(me, ZN * CN)
-        self.z = lax.rem(lax.div(me, CN), ZN)
-        self.c = lax.rem(me, CN)
-        sign = 1 + 2 * self.c
-        self.ys = [lax.rem(self.y + sign * k, YN) * (ZN * CN) for k in range(YN)]
-        self.zs = [lax.rem(self.z + sign * k, ZN) * CN for k in range(ZN)]
-        self.cs = [self.c, 1 - self.c]
-        self.sign = sign
-
-    def node(self, dy, dz, dc):
-        return self.ys[dy] + self.zs[dz] + self.cs[dc]
+        y = lax.div(me, SIDE * CN)
+        z = lax.rem(lax.div(me, CN), SIDE)
+        c = lax.rem(me, CN)
+        self.me, self.c = me, c
+        self.a, self.b = y + c * (z - y), z + c * (y - z)
+        self.stride_a = SIDE * CN - (SIDE * CN - CN) * c
+        self.stride_b = CN + (SIDE * CN - CN) * c
+        self.sign = 1 + 2 * c
+        self.a_at = [lax.rem(self.a + self.sign * k, SIDE) for k in range(SIDE)]
+        self.b_at = [lax.rem(self.b + self.sign * k, SIDE) for k in range(SIDE)]
+        self.a_nodes = [v * self.stride_a for v in self.a_at]
+        self.b_nodes = [v * self.stride_b for v in self.b_at]
+        self.cs = [c, 1 - c]
+
+    def node(self, da, db, dc):
+        return self.a_nodes[da] + self.b_nodes[db] + self.cs[dc]
 
     def peer(self, t):
         return self.node(*SLOT_OFFSETS[t])
@@ -86,9 +91,10 @@
     def peer_in(self, k, j):
         group = GROUPS[k]
         if group[0] == ROW:
-            return self.ys[group[1]] + lax.rem(self.z + self.sign * j, ZN) * CN + self.cs[group[2]]
-        y = lax.rem(self.y + self.sign * (1 + 2 * lax.div(j, 2)), YN)
-        return y * (ZN * CN) + self.zs[group[1]] + lax.rem(self.c + lax.rem(j, 2), CN)
+            b = lax.rem(self.b + self.sign * j, SIDE)
+            return self.a_nodes[group[1]] + b * self.stride_b + self.cs[group[2]]
+        a = lax.rem(self.a + self.sign * (1 + 2 * lax.div(j, 2)), SIDE)
+        return a * self.stride_a + self.b_nodes[group[1]] + lax.rem(self.c + lax.rem(j, 2), CN)
 
 
 def each(slots, body):
@@ -108,14 +114,14 @@
     papers, counts, authors, w_hbm, go_hbm, pf_hbm, sa_hbm,
     ga, gr, gs,
     w, wt, g, feat, agg, table, rows, send, relay, recv, late_send, late_recv, auth, acc,
-    racc, sacc, wg, csend, crecv, yfar_send, yfar_recv, ynear_send, ynear_recv, own_sum, zsend, zrecv,
+    racc, sacc, wg, csend, crecv, afar_send, afar_recv, anear_send, anear_recv, own_sum, b_send, b_recv,
     far_send, far_recv, near_send, near_recv,
     wsem, gsem, fsem, asem, au_s, au_r, ms_s, ms_r, rl_s, rl_r, lt_s, lt_r,
-    c_s, c_r, yf_s, yf_r, yn_s, yn_r, z_s, z_r, far_s, far_r, near_s, near_r,
+    c_s, c_r, af_s, af_r, an_s, an_r, b_s, b_r, far_s, far_r, near_s, near_r,
 ):
     at = Place()
     q = lax.axis_index("rel")
-    me, y, z, c, node = at.me, at.y, at.z, at.c, at.node
+    me, c, node = at.me, at.c, at.node
 
     def g_copy(k):
         return pltpu.make_async_copy(go_hbm.at[chunk(k)], g.at[chunk(k)], gsem.at[k])
@@ -147,6 +153,20 @@
 
     w_copy.wait()
     wt[...] = w[...].astype(F32).T.astype(BF16)
+
+    pl.semaphore_wait(barrier, NODES - 1 + 2)
+
+    def remote(src, dst, sems, i, to):
+        return pltpu.make_async_remote_copy(
+            src_ref=src, dst_ref=dst, send_sem=sems[0].at[i], recv_sem=sems[1].at[i],
+            device_id={"nodes": to}, device_id_type=MESH,
+        )
+
+    def auth_copy(t):
+        return remote(authors.at[at.peer(t)], auth.at[t], (au_s, au_r), t, at.peer(t))
+
+    each(OTHERS, lambda t: auth_copy(t).start())
+    auth[HERE] = authors[me]
 
     def back_step(k):
         g_copy(k).wait()
@@ -159,17 +179,6 @@
 
     loop(0, CHUNKS, back_step)
     loop(0, CHUNKS, load_rest)
-    pl.semaphore_wait(barrier, NODES - 1 + 2)
-
-    def remote(src, dst, sems, i, to):
-        return pltpu.make_async_remote_copy(
-            src_ref=src, dst_ref=dst, send_sem=sems[0].at[i], recv_sem=sems[1].at[i],
-            device_id={"nodes": to}, device_id_type=MESH,
-        )
-
-    def auth_copy(t):
-        return remote(authors.at[at.peer(t)], auth.at[t], (au_s, au_r), t, at.peer(t))
-
     def relay_copy(t):
         i = RELAYED.index(t)
         return remote(send.at[block(t)], relay.at[block(i)], (rl_s, rl_r), i, node(*first_hop(t)))
@@ -220,8 +229,6 @@
             late_send[1, block(k * 4 + j), :] = right
 
         loop(0, 4, late_step)
-    each(OTHERS, lambda t: auth_copy(t).start())
-    auth[HERE] = authors[me]
     recv[block(HERE), :] = send[block(HERE), :]
 
     racc[...] = jnp.zeros_like(racc)
@@ -245,13 +252,14 @@
 
     sacc_t = sacc[...].T
     for n in range(NODES):
-        co, yz = n % CN, n // CN
+        co, y, z = n % CN, n // CN // SIDE, n // CN % SIDE
+        ab = (y * SIDE + z, z * SIDE + y)[co]
         for k in range(8):
-            wg[co, yz, 8 * k:8 * k + 8, :] = racc[8 * n:8 * n + 8, 128 * k:128 * k + 128]
+            wg[co, ab, 8 * k:8 * k + 8, :] = racc[8 * n:8 * n + 8, 128 * k:128 * k + 128]
         for i in range(3):
             for h in range(2):
                 r0 = 64 + (2 * i + h) * 8
-                wg[co, yz, r0:r0 + 8, :] = sacc_t[24 * n + 8 * i:24 * n + 8 * i + 8, 128 * h:128 * h + 128]
+                wg[co, ab, r0:r0 + 8, :] = sacc_t[24 * n + 8 * i:24 * n + 8 * i + 8, 128 * h:128 * h + 128]
 
     core_copy = pltpu.make_async_remote_copy(
         src_ref=csend, dst_ref=crecv, send_sem=c_s, recv_sem=c_r,
@@ -261,7 +269,7 @@
     def core_round(i):
         csend[i] = wg[1 - c, i].astype(BF16)
 
-    loop(0, YN * ZN, core_round)
+    loop(0, SIDE * SIDE, core_round)
     core_copy.start()
     for h in range(2):
         each(range(LATE), lambda i: late_copy(h, i).start())
@@ -297,67 +305,65 @@
             late_copy(h, s * PER_SCAT + u).wait_recv()
         add_rows(WHOLE + s * PER_SCAT, late_recv[h, group(s), :], slice(h * HALF, h * HALF + HALF))
 
-    def y_to(d):
-        return lax.div(at.ys[1 + 2 * d], ZN * CN)
-
     def pair(to, p):
-        return to * ZN + 2 * p
-
-    def yfar_copy(d):
-        return remote(yfar_send.at[d], yfar_recv.at[d], (yf_s, yf_r), d, node(1 + 2 * d, 0, 0))
-
-    def ynear_copy(d, p):
+        return to * SIDE + 2 * p
+
+    def afar_copy(d):
+        return remote(afar_send.at[d], afar_recv.at[d], (af_s, af_r), d, node(1 + 2 * d, 0, 0))
+
+    def anear_copy(d, p):
         return remote(
-            ynear_send.at[d, p], ynear_recv.at[d, p], (yn_s, yn_r), 2 * d + p, node(1 + 2 * d, 0, 0)
-        )
-
-    def z_copy(d):
-        to = lax.div(at.zs[d], CN)
-        return remote(zsend.at[to], zrecv.at[d - 1], (z_s, z_r), d - 1, node(0, d, 0))
+            anear_send.at[d, p], anear_recv.at[d, p], (an_s, an_r), 2 * d + p, node(1 + 2 * d, 0, 0)
+        )
+
+    def b_copy(d):
+        return remote(
+            b_send.at[at.b_at[d]], b_recv.at[d - 1], (b_s, b_r), d - 1, node(0, d, 0)
+        )
 
     def core_sum(i):
         wg[c, i] = wg[c, i] + crecv[i].astype(F32)
 
-    def y_first():
+    def a_first():
         core_copy.wait_recv()
-        loop(0, YN * ZN, core_sum)
+        loop(0, SIDE * SIDE, core_sum)
         for d in range(2):
             for i in range(2):
-                yfar_send[d, i] = wg[c, pair(lax.rem(y + 2, YN), d) + i].astype(BF16)
-            yfar_copy(d).start()
+                afar_send[d, i] = wg[c, pair(at.a_at[2], d) + i].astype(BF16)
+            afar_copy(d).start()
         for d in range(2):
             for i in range(2):
-                ynear_send[d, 1 - d, i] = wg[c, pair(y_to(d), 1 - d) + i].astype(BF16)
-            ynear_copy(d, 1 - d).start()
-
-    def y_second():
-        for d in range(2):
-            yfar_copy(d).wait_recv()
+                anear_send[d, 1 - d, i] = wg[c, pair(at.a_at[1 + 2 * d], 1 - d) + i].astype(BF16)
+            anear_copy(d, 1 - d).start()
+
+    def a_second():
+        for d in range(2):
+            afar_copy(d).wait_recv()
             for i in range(2):
-                total = wg[c, pair(y_to(d), d) + i] + yfar_recv[d, i].astype(F32)
-                ynear_send[d, d, i] = total.astype(BF16)
-            ynear_copy(d, d).start()
-
-    def z_first():
+                total = wg[c, pair(at.a_at[1 + 2 * d], d) + i] + afar_recv[d, i].astype(F32)
+                anear_send[d, d, i] = total.astype(BF16)
+            anear_copy(d, d).start()
+
+    def b_first():
         for p in range(2):
             for d in range(2):
-                ynear_copy(d, p).wait_recv()
+                anear_copy(d, p).wait_recv()
             for i in range(2):
                 total = (
-                    wg[c, pair(y, p) + i]
-                    + ynear_recv[0, p, i].astype(F32) + ynear_recv[1, p, i].astype(F32)
+                    wg[c, pair(at.a, p) + i]
+                    + anear_recv[0, p, i].astype(F32) + anear_recv[1, p, i].astype(F32)
                 )
                 own_sum[2 * p + i] = total
-                zsend[2 * p + i] = total.astype(BF16)
-        for d in range(1, ZN):
-            z_copy(d).start()
-
-    def z_last():
-        for d in range(1, ZN):
-            z_copy(d).wait_recv()
-        total = own_sum[z]
-        for d in range(ZN - 1):
-            total = total + zrecv[d].astype(F32)
+                b_send[2 * p + i] = total.astype(BF16)
+        for d in range(1, SIDE):
+            b_copy(d).start()
+
+    def b_last():
+        for d in range(1, SIDE):
+            b_copy(d).wait_recv()
+        total = own_sum[at.b]
+        for d in range(SIDE - 1):
+            total = total + b_recv[d].astype(F32)
         for k in range(8):
             gr[:, 128 * k:128 * k + 128] = total[8 * k:8 * k + 8, :]
         for i in range(3):
@@ -366,7 +372,7 @@
                 gs[8 * i:8 * i + 8, 128 * h:128 * h + 128] = total[r0:r0 + 8, :]
 
     def towards(d):
-        return lax.rem(q + (1, REL - 1)[d], REL)
+        return lax.rem(q + (1, REL - 1)[d] * at.sign, REL)
 
     def rows_of(owner, p):
         return pl.ds(pl.multiple_of(owner * OWN + p * PART, PART), PART)
@@ -412,23 +418,23 @@
                 + near_recv[h, 0, p].astype(F32) + near_recv[h, 1, p].astype(F32)
             )
 
+    scatter(4)
     scatter(3)
     scatter(5)
-    scatter(4)
-    y_first()
+    a_first()
     scatter(0)
     scatter(1)
-    y_second()
+    a_second()
     scatter(2)
     scatter_late(0, 0)
     scatter_late(0, 1)
     rel_first(0)
-    z_first()
+    b_first()
     scatter_late(1, 0)
     rel_second(0)
     scatter_late(1, 1)
     rel_first(1)
-    z_last()
+    b_last()
     rel_last(0)
     rel_second(1)
     rel_last(1)
@@ -444,11 +450,11 @@
             for p in range(2):
                 near_copy(h, d, p).wait_send()
     for d in range(2):
-        yfar_copy(d).wait_send()
+        afar_copy(d).wait_send()
         for p in range(2):
-            ynear_copy(d, p).wait_send()
-    for d in range(1, ZN):
-        z_copy(d).wait_send()
+            anear_copy(d, p).wait_send()
+    for d in range(1, SIDE):
+        b_copy(d).wait_send()
 
 
 def hand_over(a, b, c, ao, bo, co):
@@ -491,16 +497,16 @@
             pltpu.VMEM((GROUP, AUTH_W), F32),
             pltpu.VMEM((AUTH_W, OUT_W), F32),
             pltpu.VMEM((AUTH_W, PAPER_W), F32),
-            pltpu.VMEM((CN, YN * ZN, PIECE, 128), F32),
-            pltpu.VMEM((YN * ZN, PIECE, 128), BF16),
-            pltpu.VMEM((YN * ZN, PIECE, 128), BF16),
+            pltpu.VMEM((CN, SIDE * SIDE, PIECE, 128), F32),
+            pltpu.VMEM((SIDE * SIDE, PIECE, 128), BF16),
+            pltpu.VMEM((SIDE * SIDE, PIECE, 128), BF16),
             pltpu.VMEM((2, 2, PIECE, 128), BF16),
             pltpu.VMEM((2, 2, PIECE, 128), BF16),
             pltpu.VMEM((2, 2, 2, PIECE, 128), BF16),
             pltpu.VMEM((2, 2, 2, PIECE, 128), BF16),
-            pltpu.VMEM((ZN, PIECE, 128), F32),
-            pltpu.VMEM((ZN, PIECE, 128), BF16),
-            pltpu.VMEM((ZN - 1, PIECE, 128), BF16),
+            pltpu.VMEM((SIDE, PIECE, 128), F32),
+            pltpu.VMEM((SIDE, PIECE, 128), BF16),
+            pltpu.VMEM((SIDE - 1, PIECE, 128), BF16),
             pltpu.VMEM((2, 2, PART, HALF), BF16),
             pltpu.VMEM((2, 2, PART, HALF), BF16),
             pltpu.VMEM((2, 2, 2, PART, HALF), BF16),

time: 65.3 us -> 60.9 us (0.933)
  Pallas kernels: 64.5 us -> 60.1 us
    pallas_call x1, Pallas kernels: 62.6 us -> 58.2 us  [on_device(): pl.pallas_call(kernel, out_shape=(jax.ShapeDtypeStruct((OWN, AUTH_W), F32...]
where the time goes in v2:
time: 60.9 us; the launch traced here: 60.7 us
  Pallas kernels  60.1 us (99%)
  between operations  0.64 us (1%)
    pallas_call x1, Pallas kernels, on_device(): pl.pallas_call(kernel, out_shape=(jax.ShapeDtypeStruct((OWN, AUTH_W), F32...  58.2 us
    pallas_call x1, Pallas kernels, on_device(): pl.pallas_call(hand_over, out_shape=tuple((jax.ShapeDtypeStruct(v.shape,...  1.9 us

profile of v2, /device:TPU:0, one launch (start us, length us, event | category | flops | bytes accessed | tf_op | source)
XLA Modules:
  0.0 60.7 jit_solution(8848694925403895812)
XLA Ops:
  0.6 58.2 %shard_map.94 = (f32[512,256]{1,0:T(8,128)}, f32[8,1024]{1,0:T(8,128)}, f32[24,256]{1,0:T(8,128)}) custom-call(s32[32,128]{1,0:T(8,128)} %bitcast.8, s32[32]{0:T(128)} %bitcast.10, s32[32,1,128]{2,1,0:T(1,128)} %bitcast.9, bf16[256,1024]{1,0:T(8,128)(2,1)} %bitcast.7, bf16[4608,1024]{1,0:T(8,128)(2,1)} %go_hbm.1, bf16[4608,768]{1,0:T(8,128)(2,1)} %pf_hbm.1, ...), custom_call_target="tpu_custom_call" | custom-call | tf_op jit(solution)/shard_map/pallas_call | solution.py:474
  58.8 1.9 %shard_map.95 = (f32[512,256]{1,0:T(8,128)}, f32[8,1024]{1,0:T(8,128)}, f32[24,256]{1,0:T(8,128)}) custom-call(f32[512,256]{1,0:T(8,128)} %get-tuple-element.9.a, f32[8,1024]{1,0:T(8,128)} %get-tuple-element.10.b, f32[24,256]{1,0:T(8,128)} %get-tuple-element.11.c), custom_call_target="tpu_custom_call" | custom-call | tf_op jit(solution)/shard_map/pallas_call | solution.py:527

commit v3 on v2

--- a/solution.py
+++ b/solution.py
@@ -20,7 +20,7 @@
 PER_SCAT = 4
 SCAT_ROWS = 1024
 WHOLE = 24
-LATE = NODES - WHOLE
+COPIES = 39
 HALF = AUTH_W // 2
 PART = OWN // 2
 
@@ -29,40 +29,10 @@
     return pl.ds(pl.multiple_of(k * CHUNK, CHUNK), CHUNK)
 
 
-def block(t):
-    if isinstance(t, int):
-        return pl.ds(t * SLOTS, SLOTS)
-    return pl.ds(pl.multiple_of(t * SLOTS, SLOTS), SLOTS)
-
-
-ROW, COLUMN = 0, 1
-GROUPS = [(ROW, 2, 0), (COLUMN, 2), (ROW, 2, 1), (ROW, 0, 0), (COLUMN, 0), (ROW, 0, 1), (COLUMN, 1), (COLUMN, 3)]
-
-
-def in_group(group, j):
-    if group[0] == ROW:
-        return group[1], j, group[2]
-    return 1 + 2 * (j // 2), group[1], j % 2
-
-
-SLOT_OFFSETS = [in_group(group, j) for group in GROUPS for j in range(4)]
-HERE = SLOT_OFFSETS.index((0, 0, 0))
-OTHERS = [t for t in range(NODES) if t != HERE]
-RELAYED = [t for t in OTHERS if 2 in SLOT_OFFSETS[t][:2]]
-DIRECT = [t for t in OTHERS if t < WHOLE and t not in RELAYED]
-
-
-def first_hop(t):
-    da, db, dc = SLOT_OFFSETS[t]
-    ha = (1 if db < 2 else 3) if da == 2 else 0
-    hb = (1 if da in (1, 2) else 3) if db == 2 else 0
-    return ha, hb, 0
-
-
-def second_hop(t):
-    da, db, dc = SLOT_OFFSETS[t]
-    ha, hb, _ = first_hop(t)
-    return (da - ha) % SIDE, (db - hb) % SIDE, dc
+DB = (0, 1, 3, 2)
+SLOT_OFFSETS = [(da, db, dc) for db in DB for dc in range(CN) for da in range(SIDE)]
+HERE = 0
+OTHERS = range(1, NODES)
 
 
 class Place:
@@ -88,13 +58,10 @@
     def peer(self, t):
         return self.node(*SLOT_OFFSETS[t])
 
-    def peer_in(self, k, j):
-        group = GROUPS[k]
-        if group[0] == ROW:
-            b = lax.rem(self.b + self.sign * j, SIDE)
-            return self.a_nodes[group[1]] + b * self.stride_b + self.cs[group[2]]
-        a = lax.rem(self.a + self.sign * (1 + 2 * lax.div(j, 2)), SIDE)
-        return a * self.stride_a + self.b_nodes[group[1]] + lax.rem(self.c + lax.rem(j, 2), CN)
+    def anywhere(self, da, db, dc):
+        a = lax.rem(self.a + self.sign * da, SIDE)
+        b = lax.rem(self.b + self.sign * db, SIDE)
+        return a * self.stride_a + b * self.stride_b + lax.rem(self.c + dc, CN)
 
 
 def each(slots, body):
@@ -113,10 +80,11 @@
 def kernel(
     papers, counts, authors, w_hbm, go_hbm, pf_hbm, sa_hbm,
     ga, gr, gs,
-    w, wt, g, feat, agg, table, rows, send, relay, recv, late_send, late_recv, auth, acc,
+    w, wt, g, feat, agg, table, rows, send, mid, recv, relay_p, relay_m, relay_late,
+    late_send, late_mid, late_relay, late_recv, auth, acc,
     racc, sacc, wg, csend, crecv, afar_send, afar_recv, anear_send, anear_recv, own_sum, b_send, b_recv,
     far_send, far_recv, near_send, near_recv,
-    wsem, gsem, fsem, asem, au_s, au_r, ms_s, ms_r, rl_s, rl_r, lt_s, lt_r,
+    wsem, gsem, fsem, asem, au_s, au_r, ms_s, ms_r,
     c_s, c_r, af_s, af_r, an_s, an_r, b_s, b_r, far_s, far_r, near_s, near_r,
 ):
     at = Place()
@@ -179,22 +147,44 @@
 
     loop(0, CHUNKS, back_step)
     loop(0, CHUNKS, load_rest)
-    def relay_copy(t):
-        i = RELAYED.index(t)
-        return remote(send.at[block(t)], relay.at[block(i)], (rl_s, rl_r), i, node(*first_hop(t)))
-
-    def msg_copy(t):
-        if t in RELAYED:
-            source, to = relay.at[block(RELAYED.index(t))], node(*second_hop(t))
-        else:
-            source, to = send.at[block(t)], at.peer(t)
-        return remote(source, recv.at[block(t)], (ms_s, ms_r), t, to)
-
-    def late_copy(h, i):
-        return remote(
-            late_send.at[h, block(i)], late_recv.at[h, block(i)],
-            (lt_s, lt_r), h * LATE + i, at.peer(WHOLE + i),
-        )
+    copies = {}
+
+    def link(key, src, dst, *offset):
+        copies[key] = remote(src, dst, (ms_s, ms_r), len(copies), node(*offset))
+
+    def start(*keys):
+        for key in keys:
+            copies[key].start()
+
+    def arrived(*keys):
+        for key in keys:
+            copies[key].wait_recv()
+
+    link("a2+", send.at[0:2, :, 2], relay_p, 1, 0, 0)
+    link("a2-", send.at[2, :, 2], relay_m, 3, 0, 0)
+    link("a2late", late_send.at[:, :, 2], relay_late, 3, 0, 0)
+    for da in (1, 3):
+        link(("a", da), send.at[1:3, :, da], mid.at[1:3, :, da], da, 0, 0)
+        link(("alate", da), late_send.at[:, :, da], late_mid.at[:, :, da], da, 0, 0)
+        for dc in range(CN):
+            link(("direct", da, dc), send.at[0, dc, da], recv.at[0, dc, da], da, 0, dc)
+    link("core", send.at[0, 1, 0], recv.at[0, 1, 0], 0, 0, 1)
+    link("f+", relay_p.at[1], mid.at[1, :, 2], 1, 0, 0)
+    for dc in range(CN):
+        link(("f0", dc), relay_p.at[0, dc], recv.at[0, dc, 2], 1, 0, dc)
+    link("f-", relay_m, mid.at[2, :, 2], 3, 0, 0)
+    link("flate", relay_late, late_mid.at[:, :, 2], 3, 0, 0)
+    for i, db in ((1, 1), (2, 3)):
+        for dc in range(CN):
+            link(("own", i, dc), send.at[i, dc, 0], recv.at[i, dc, 0], 0, db, dc)
+            link(("mid", i, dc), mid.at[i, dc, 1:4], recv.at[i, dc, 1:4], 0, db, dc)
+    for h in range(2):
+        link(("l0", h), late_send.at[h, :, 0], late_relay.at[h, :, 0], 0, 1, 0)
+        link(("l1", h), late_mid.at[h, :, 1], late_relay.at[h, :, 1], 0, 1, 0)
+        link(("l2", h), late_mid.at[h, :, 2:4], late_relay.at[h, :, 2:4], 0, 3, 0)
+        for dc in range(CN):
+            link(("lf+", h, dc), late_relay.at[h, dc, 0:2], late_recv.at[h, dc, 0:2], 0, 1, dc)
+            link(("lf-", h, dc), late_relay.at[h, dc, 2:4], late_recv.at[h, dc, 2:4], 0, 3, dc)
 
     def gather(b):
         for u in range(SLOTS):
@@ -208,28 +198,57 @@
             for h in range(2)
         ]
 
-    for k in range(WHOLE // 4):
-
-        def whole_step(j):
-            left, right = gather(at.peer_in(k, j))
-            send[block(k * 4 + j), :HALF] = left
-            send[block(k * 4 + j), HALF:] = right
-
-        loop(0, 4, whole_step)
-        for t in range(k * 4, k * 4 + 4):
-            if t in RELAYED:
-                relay_copy(t).start()
-            elif t != HERE:
-                msg_copy(t).start()
-    for k in range(LATE // 4):
-
-        def late_step(j):
-            left, right = gather(at.peer_in(WHOLE // 4 + k, j))
-            late_send[0, block(k * 4 + j), :] = left
-            late_send[1, block(k * 4 + j), :] = right
-
-        loop(0, 4, late_step)
-    recv[block(HERE), :] = send[block(HERE), :]
+    def whole(i, db, dc, da):
+        left, right = gather(at.anywhere(da, db, dc))
+        send[i, dc, da, :, :HALF] = left
+        send[i, dc, da, :, HALF:] = right
+
+    def late(dc, da):
+        left, right = gather(at.anywhere(da, 2, dc))
+        late_send[0, dc, da] = left
+        late_send[1, dc, da] = right
+
+    def two(j):
+        return lax.div(j, 2), lax.rem(j, 2)
+
+    def sides(da):
+        def body(j):
+            i, dc = two(j)
+            whole(1 + i, 1 + 2 * i, dc, da)
+
+        loop(0, 4, body)
+
+    def body_a2(j):
+        i, dc = two(j)
+        whole(i, i, dc, 2)
+
+    def body_direct(j):
+        i, dc = two(j)
+        whole(0, 0, dc, 1 + 2 * i)
+
+    def body_late(j):
+        i, dc = two(j)
+        late(dc, 1 + 2 * i)
+
+    loop(0, 4, body_a2)
+    start("a2+")
+    loop(0, 2, lambda dc: whole(2, 3, dc, 2))
+    loop(0, 2, lambda dc: late(dc, 2))
+    start("a2-", "a2late")
+    for da in (1, 3):
+        sides(da)
+        start(("a", da))
+    loop(0, 4, body_late)
+    start(("alate", 1), ("alate", 3))
+    loop(0, 4, body_direct)
+    start(*[("direct", da, dc) for da in (1, 3) for dc in range(CN)])
+    loop(0, 2, lambda dc: late(dc, 0))
+    start(("l0", 0), ("l0", 1))
+    sides(0)
+    start(*[("own", i, dc) for i in (1, 2) for dc in range(CN)])
+    loop(0, 2, lambda dc: whole(0, 0, dc, 0))
+    start("core")
+    recv[0, 0, 0] = send[0, 0, 0]
 
     racc[...] = jnp.zeros_like(racc)
     sacc[...] = jnp.zeros_like(sacc)
@@ -242,13 +261,13 @@
         racc[...] += lax.dot_general(agg[chunk(k), :], g[chunk(k), :], over0, **DOTS)
         sacc[...] += lax.dot_general(g[chunk(k), cols], feat[chunk(k), :], over0, **DOTS)
 
-    def forward(t):
-        relay_copy(t).wait_recv()
-        msg_copy(t).start()
-
-    loop(0, 2, grads_step)
-    each(RELAYED, forward)
-    loop(2, CHUNKS, grads_step)
+    loop(0, 1, grads_step)
+    arrived("a2+", "a2-", "a2late")
+    start("flate", "f-", "f+", ("f0", 0), ("f0", 1))
+    loop(1, CHUNKS, grads_step)
+    arrived(("a", 1), ("a", 3), ("alate", 1), ("alate", 3), "flate", "f-", "f+")
+    start(*[(key, h) for h in range(2) for key in ("l1", "l2")])
+    start(*[("mid", i, dc) for dc in range(CN) for i in (1, 2)])
 
     sacc_t = sacc[...].T
     for n in range(NODES):
@@ -271,8 +290,6 @@
 
     loop(0, SIDE * SIDE, core_round)
     core_copy.start()
-    for h in range(2):
-        each(range(LATE), lambda i: late_copy(h, i).start())
 
     acc[...] = jnp.zeros_like(acc)
     each(OTHERS, lambda t: auth_copy(t).wait_recv())
@@ -290,20 +307,23 @@
 
         loop(0, GROUP // SCAT_ROWS, some)
 
-    def group(s):
-        width = PER_SCAT * SLOTS
-        return pl.ds(pl.multiple_of(s * width, width), width)
-
-    def scatter(s):
-        for u in range(PER_SCAT):
-            if s * PER_SCAT + u != HERE:
-                msg_copy(s * PER_SCAT + u).wait_recv()
-        add_rows(s * PER_SCAT, recv[group(s), :], slice(None))
-
-    def scatter_late(h, s):
-        for u in range(PER_SCAT):
-            late_copy(h, s * PER_SCAT + u).wait_recv()
-        add_rows(WHOLE + s * PER_SCAT, late_recv[h, group(s), :], slice(h * HALF, h * HALF + HALF))
+    def scatter(i, dc):
+        if i == 0:
+            arrived(("direct", 1, dc), ("direct", 3, dc), ("f0", dc))
+            if dc == 1:
+                arrived("core")
+        else:
+            arrived(("own", i, dc), ("mid", i, dc))
+        add_rows((i * CN + dc) * 4, recv[i, dc].reshape(4 * SLOTS, AUTH_W), slice(None))
+
+    def scatter_late(h, dc):
+        arrived(("lf+", h, dc), ("lf-", h, dc))
+        msg = late_recv[h, dc].reshape(4 * SLOTS, HALF)
+        add_rows(WHOLE + dc * 4, msg, slice(h * HALF, h * HALF + HALF))
+
+    def forward_late(h):
+        arrived(("l0", h), ("l1", h), ("l2", h))
+        start(*[(key, h, dc) for dc in range(CN) for key in ("lf+", "lf-")])
 
     def pair(to, p):
         return to * SIDE + 2 * p
@@ -418,14 +438,16 @@
                 + near_recv[h, 0, p].astype(F32) + near_recv[h, 1, p].astype(F32)
             )
 
-    scatter(4)
-    scatter(3)
-    scatter(5)
+    scatter(0, 0)
+    scatter(0, 1)
+    forward_late(0)
+    forward_late(1)
     a_first()
-    scatter(0)
-    scatter(1)
+    scatter(1, 0)
+    scatter(2, 0)
     a_second()
-    scatter(2)
+    scatter(1, 1)
+    scatter(2, 1)
     scatter_late(0, 0)
     scatter_late(0, 1)
     rel_first(0)
@@ -441,10 +463,9 @@
 
     core_copy.wait_send()
     each(OTHERS, lambda t: auth_copy(t).wait_send())
-    each(RELAYED, lambda t: relay_copy(t).wait_send())
-    each(RELAYED + DIRECT, lambda t: msg_copy(t).wait_send())
+    for copy in copies.values():
+        copy.wait_send()
     for h in range(2):
-        each(range(LATE), lambda i: late_copy(h, i).wait_send())
         for d in range(2):
             far_copy(h, d).wait_send()
             for p in range(2):
@@ -469,8 +490,8 @@
     hbm = pl.BlockSpec(memory_space=pl.ANY)
     dma = pltpu.SemaphoreType.DMA
     limit = 56 * 1024 * 1024
-    whole = (WHOLE * SLOTS, AUTH_W)
-    late = (2, LATE * SLOTS, HALF)
+    whole = (3, CN, SIDE, SLOTS, AUTH_W)
+    late = (2, CN, SIDE, SLOTS, HALF)
     ga, gr, gs = pl.pallas_call(
         kernel,
         out_shape=(
@@ -489,8 +510,13 @@
             pltpu.VMEM((2 * PAPERS, HALF), F32),
             pltpu.VMEM((2 * SLOTS, HALF), F32),
             pltpu.VMEM(whole, BF16),
-            pltpu.VMEM((len(RELAYED) * SLOTS, AUTH_W), BF16),
             pltpu.VMEM(whole, BF16),
+            pltpu.VMEM(whole, BF16),
+            pltpu.VMEM((2, CN, SLOTS, AUTH_W), BF16),
+            pltpu.VMEM((CN, SLOTS, AUTH_W), BF16),
+            pltpu.VMEM((2, CN, SLOTS, HALF), BF16),
+            pltpu.VMEM(late, BF16),
+            pltpu.VMEM(late, BF16),
             pltpu.VMEM(late, BF16),
             pltpu.VMEM(late, BF16),
             pltpu.VMEM((NODES, 1, SLOTS), jnp.int32),
@@ -512,8 +538,7 @@
             pltpu.VMEM((2, 2, 2, PART, HALF), BF16),
             pltpu.VMEM((2, 2, 2, PART, HALF), BF16),
             dma, dma((CHUNKS,)), dma((CHUNKS,)), dma((CHUNKS,)),
-            dma((NODES,)), dma((NODES,)), dma((WHOLE,)), dma((WHOLE,)),
-            dma((len(RELAYED),)), dma((len(RELAYED),)), dma((2 * LATE,)), dma((2 * LATE,)),
+            dma((NODES,)), dma((NODES,)), dma((COPIES,)), dma((COPIES,)),
             dma, dma, dma((2,)), dma((2,)), dma((4,)), dma((4,)), dma((3,)), dma((3,)),
             dma((2, 2)), dma((2, 2)), dma((2, 2, 2)), dma((2, 2, 2)),
         ],

time: 60.9 us -> 63 us (1.034)
  Pallas kernels: 60.1 us -> 62.2 us
    pallas_call x1, Pallas kernels: 58.2 us -> 60.3 us  [on_device(): pl.pallas_call(kernel, out_shape=(jax.ShapeDtypeStruct((OWN, AUTH_W), F32...]
where the time goes in v3:
time: 63 us; the launch traced here: 62.8 us
  Pallas kernels  62.2 us (99%)
  between operations  0.64 us (1%)
    pallas_call x1, Pallas kernels, on_device(): pl.pallas_call(kernel, out_shape=(jax.ShapeDtypeStruct((OWN, AUTH_W), F32...  60.3 us
    pallas_call x1, Pallas kernels, on_device(): pl.pallas_call(hand_over, out_shape=tuple((jax.ShapeDtypeStruct(v.shape,...  1.9 us

profile of v3, /device:TPU:0, one launch (start us, length us, event | category | flops | bytes accessed | tf_op | source)
XLA Modules:
  0.0 62.8 jit_solution(1336829289828992538)
XLA Ops:
  0.6 60.3 %shard_map.94 = (f32[512,256]{1,0:T(8,128)}, f32[8,1024]{1,0:T(8,128)}, f32[24,256]{1,0:T(8,128)}) custom-call(s32[32,128]{1,0:T(8,128)} %bitcast.8, s32[32]{0:T(128)} %bitcast.10, s32[32,1,128]{2,1,0:T(1,128)} %bitcast.9, bf16[256,1024]{1,0:T(8,128)(2,1)} %bitcast.7, bf16[4608,1024]{1,0:T(8,128)(2,1)} %go_hbm.1, bf16[4608,768]{1,0:T(8,128)(2,1)} %pf_hbm.1, ...), custom_call_target="tpu_custom_call" | custom-call | tf_op jit(solution)/shard_map/pallas_call | solution.py:495
  60.9 1.9 %shard_map.95 = (f32[512,256]{1,0:T(8,128)}, f32[8,1024]{1,0:T(8,128)}, f32[24,256]{1,0:T(8,128)}) custom-call(f32[512,256]{1,0:T(8,128)} %get-tuple-element.9.a, f32[8,1024]{1,0:T(8,128)} %get-tuple-element.10.b, f32[24,256]{1,0:T(8,128)} %get-tuple-element.11.c), custom_call_target="tpu_custom_call" | custom-call | tf_op jit(solution)/shard_map/pallas_call | solution.py:552

commit v4 on v2

--- a/solution.py
+++ b/solution.py
@@ -16,10 +16,13 @@
 SLOTS, GROUP, OWN = 128, 2048, 512
 CHUNK = 768
 CHUNKS = PAPERS // CHUNK
+STEP = 384
+STEPS = PAPERS // STEP
+AHEAD = 5
 PIECE = 112
 PER_SCAT = 4
 SCAT_ROWS = 1024
-WHOLE = 24
+WHOLE = 20
 LATE = NODES - WHOLE
 HALF = AUTH_W // 2
 PART = OWN // 2
@@ -36,7 +39,7 @@
 
 
 ROW, COLUMN = 0, 1
-GROUPS = [(ROW, 2, 0), (COLUMN, 2), (ROW, 2, 1), (ROW, 0, 0), (COLUMN, 0), (ROW, 0, 1), (COLUMN, 1), (COLUMN, 3)]
+GROUPS = [(ROW, 2, 0), (COLUMN, 2), (ROW, 2, 1), (ROW, 0, 0), (ROW, 0, 1), (COLUMN, 0), (COLUMN, 1), (COLUMN, 3)]
 
 
 def in_group(group, j):
@@ -124,7 +127,8 @@
     me, c, node = at.me, at.c, at.node
 
     def g_copy(k):
-        return pltpu.make_async_copy(go_hbm.at[chunk(k)], g.at[chunk(k)], gsem.at[k])
+        span = pl.ds(pl.multiple_of(k * STEP, STEP), STEP)
+        return pltpu.make_async_copy(go_hbm.at[span], g.at[span], gsem.at[k])
 
     def f_copy(k):
         return pltpu.make_async_copy(pf_hbm.at[chunk(k)], feat.at[chunk(k)], fsem.at[k])
@@ -138,7 +142,7 @@
 
     w_copy = pltpu.make_async_copy(w_hbm, w, wsem)
     w_copy.start()
-    loop(0, CHUNKS, lambda k: g_copy(k).start())
+    loop(0, AHEAD, lambda k: g_copy(k).start())
 
     barrier = pltpu.get_barrier_semaphore()
 
@@ -163,21 +167,28 @@
         )
 
     def auth_copy(t):
-        return remote(authors.at[at.peer(t)], auth.at[t], (au_s, au_r), t, at.peer(t))
-
-    each(OTHERS, lambda t: auth_copy(t).start())
-    auth[HERE] = authors[me]
+        return pltpu.make_async_remote_copy(
+            src_ref=authors.at[at.peer(t)], dst_ref=auth.at[t], send_sem=au_s, recv_sem=au_r,
+            device_id={"nodes": at.peer(t)}, device_id_type=MESH,
+        )
+
+    def all_authors(sem):
+        rows_of_all = auth.at[0:NODES - 1]
+        pltpu.make_async_copy(rows_of_all, rows_of_all, sem).wait()
 
     def back_step(k):
         g_copy(k).wait()
-        part = CHUNK // 2
-        for m in range(2):
-            lo = k * CHUNK + m * part
-            back = jnp.dot(g[pl.ds(pl.multiple_of(lo, part), part), :], wt[...], **DOTS)
-            for h in range(2):
-                table[pl.ds(2 * lo + h, part, stride=2), :] = back[:, h * HALF:h * HALF + HALF]
-
-    loop(0, CHUNKS, back_step)
+
+        @pl.when(k + AHEAD < STEPS)
+        def _():
+            g_copy(k + AHEAD).start()
+
+        lo = pl.multiple_of(k * STEP, STEP)
+        back = jnp.dot(g[pl.ds(lo, STEP), :], wt[...], **DOTS)
+        for h in range(2):
+            table[pl.ds(2 * lo + h, STEP, stride=2), :] = back[:, h * HALF:h * HALF + HALF]
+
+    loop(0, STEPS, back_step)
     loop(0, CHUNKS, load_rest)
     def relay_copy(t):
         i = RELAYED.index(t)
@@ -229,6 +240,8 @@
             late_send[1, block(k * 4 + j), :] = right
 
         loop(0, 4, late_step)
+    each(OTHERS, lambda t: auth_copy(t).start())
+    auth[HERE] = authors[me]
     recv[block(HERE), :] = send[block(HERE), :]
 
     racc[...] = jnp.zeros_like(racc)
@@ -248,6 +261,8 @@
 
     loop(0, 2, grads_step)
     each(RELAYED, forward)
+    for h in range(2):
+        each(range(LATE), lambda i: late_copy(h, i).start())
     loop(2, CHUNKS, grads_step)
 
     sacc_t = sacc[...].T
@@ -271,11 +286,9 @@
 
     loop(0, SIDE * SIDE, core_round)
     core_copy.start()
-    for h in range(2):
-        each(range(LATE), lambda i: late_copy(h, i).start())
 
     acc[...] = jnp.zeros_like(acc)
-    each(OTHERS, lambda t: auth_copy(t).wait_recv())
+    all_authors(au_r)
 
     def add_rows(first_slot, msg, cols):
         targets = [auth[first_slot + u] for u in range(PER_SCAT)]
@@ -418,33 +431,33 @@
                 + near_recv[h, 0, p].astype(F32) + near_recv[h, 1, p].astype(F32)
             )
 
+    scatter(3)
     scatter(4)
-    scatter(3)
-    scatter(5)
-    a_first()
-    scatter(0)
-    scatter(1)
-    a_second()
-    scatter(2)
-    scatter_late(0, 0)
-    scatter_late(0, 1)
+    for i in range(3):
+        scatter(i)
+    for i in range(LATE // PER_SCAT):
+        scatter_late(0, i)
     rel_first(0)
-    b_first()
     scatter_late(1, 0)
     rel_second(0)
-    scatter_late(1, 1)
+    a_first()
+    for i in range(1, LATE // PER_SCAT):
+        scatter_late(1, i)
     rel_first(1)
-    b_last()
+    a_second()
     rel_last(0)
     rel_second(1)
-    rel_last(1)
-
-    core_copy.wait_send()
-    each(OTHERS, lambda t: auth_copy(t).wait_send())
+    b_first()
+    all_authors(au_s)
     each(RELAYED, lambda t: relay_copy(t).wait_send())
     each(RELAYED + DIRECT, lambda t: msg_copy(t).wait_send())
     for h in range(2):
         each(range(LATE), lambda i: late_copy(h, i).wait_send())
+    core_copy.wait_send()
+    b_last()
+    rel_last(1)
+
+    for h in range(2):
         for d in range(2):
             far_copy(h, d).wait_send()
             for p in range(2):
@@ -511,8 +524,8 @@
             pltpu.VMEM((2, 2, PART, HALF), BF16),
             pltpu.VMEM((2, 2, 2, PART, HALF), BF16),
             pltpu.VMEM((2, 2, 2, PART, HALF), BF16),
-            dma, dma((CHUNKS,)), dma((CHUNKS,)), dma((CHUNKS,)),
-            dma((NODES,)), dma((NODES,)), dma((WHOLE,)), dma((WHOLE,)),
+            dma, dma((STEPS,)), dma((CHUNKS,)), dma((CHUNKS,)),
+            dma, dma, dma((WHOLE,)), dma((WHOLE,)),
             dma((len(RELAYED),)), dma((len(RELAYED),)), dma((2 * LATE,)), dma((2 * LATE,)),
             dma, dma, dma((2,)), dma((2,)), dma((4,)), dma((4,)), dma((3,)), dma((3,)),
             dma((2, 2)), dma((2, 2)), dma((2, 2, 2)), dma((2, 2, 2)),

time: 60.9 us -> 59.7 us (0.980)
  Pallas kernels: 60.1 us -> 58.8 us
    pallas_call x1, Pallas kernels: 58.2 us -> 56.9 us  [on_device(): pl.pallas_call(kernel, out_shape=(jax.ShapeDtypeStruct((OWN, AUTH_W), F32...]
where the time goes in v4:
time: 59.7 us; the launch traced here: 59.5 us
  Pallas kernels  58.8 us (98%)
  between operations  0.64 us (1%)
    pallas_call x1, Pallas kernels, on_device(): pl.pallas_call(kernel, out_shape=(jax.ShapeDtypeStruct((OWN, AUTH_W), F32...  56.9 us
    pallas_call x1, Pallas kernels, on_device(): pl.pallas_call(hand_over, out_shape=tuple((jax.ShapeDtypeStruct(v.shape,...  1.9 us

profile of v4, /device:TPU:0, one launch (start us, length us, event | category | flops | bytes accessed | tf_op | source)
XLA Modules:
  0.0 59.5 jit_solution(5615112381107893172)
XLA Ops:
  0.6 56.9 %shard_map.94 = (f32[512,256]{1,0:T(8,128)}, f32[8,1024]{1,0:T(8,128)}, f32[24,256]{1,0:T(8,128)}) custom-call(s32[32,128]{1,0:T(8,128)} %bitcast.8, s32[32]{0:T(128)} %bitcast.10, s32[32,1,128]{2,1,0:T(1,128)} %bitcast.9, bf16[256,1024]{1,0:T(8,128)(2,1)} %bitcast.7, bf16[4608,1024]{1,0:T(8,128)(2,1)} %go_hbm.1, bf16[4608,768]{1,0:T(8,128)(2,1)} %pf_hbm.1, ...), custom_call_target="tpu_custom_call" | custom-call | tf_op jit(solution)/shard_map/pallas_call | solution.py:487
  57.6 1.9 %shard_map.95 = (f32[512,256]{1,0:T(8,128)}, f32[8,1024]{1,0:T(8,128)}, f32[24,256]{1,0:T(8,128)}) custom-call(f32[512,256]{1,0:T(8,128)} %get-tuple-element.9.a, f32[8,1024]{1,0:T(8,128)} %get-tuple-element.10.b, f32[24,256]{1,0:T(8,128)} %get-tuple-element.11.c), custom_call_target="tpu_custom_call" | custom-call | tf_op jit(solution)/shard_map/pallas_call | solution.py:540

commit v5 on v4

--- a/solution.py
+++ b/solution.py
@@ -116,7 +116,7 @@
 def kernel(
     papers, counts, authors, w_hbm, go_hbm, pf_hbm, sa_hbm,
     ga, gr, gs,
-    w, wt, g, feat, agg, table, rows, send, relay, recv, late_send, late_recv, auth, acc,
+    w, wt, g, feat, agg, table, rows, send, relay, recv, late_send, late_recv, late_hot, auth, acc,
     racc, sacc, wg, csend, crecv, afar_send, afar_recv, anear_send, anear_recv, own_sum, b_send, b_recv,
     far_send, far_recv, near_send, near_recv,
     wsem, gsem, fsem, asem, au_s, au_r, ms_s, ms_r, rl_s, rl_r, lt_s, lt_r,
@@ -158,8 +158,6 @@
     w_copy.wait()
     wt[...] = w[...].astype(F32).T.astype(BF16)
 
-    pl.semaphore_wait(barrier, NODES - 1 + 2)
-
     def remote(src, dst, sems, i, to):
         return pltpu.make_async_remote_copy(
             src_ref=src, dst_ref=dst, send_sem=sems[0].at[i], recv_sem=sems[1].at[i],
@@ -190,6 +188,8 @@
 
     loop(0, STEPS, back_step)
     loop(0, CHUNKS, load_rest)
+    pl.semaphore_wait(barrier, NODES - 1 + 2)
+
     def relay_copy(t):
         i = RELAYED.index(t)
         return remote(send.at[block(t)], relay.at[block(i)], (rl_s, rl_r), i, node(*first_hop(t)))
@@ -313,10 +313,13 @@
                 msg_copy(s * PER_SCAT + u).wait_recv()
         add_rows(s * PER_SCAT, recv[group(s), :], slice(None))
 
-    def scatter_late(h, s):
-        for u in range(PER_SCAT):
-            late_copy(h, s * PER_SCAT + u).wait_recv()
-        add_rows(WHOLE + s * PER_SCAT, late_recv[h, group(s), :], slice(h * HALF, h * HALF + HALF))
+    def hot_rows(m):
+        span = pl.ds(pl.multiple_of(m * 256, 256), 256)
+        ids = lax.broadcasted_iota(jnp.int32, (256, SLOTS), 0) + m * 256
+        for u in range(LATE):
+            late_hot[span, u * SLOTS:u * SLOTS + SLOTS] = jnp.where(
+                ids == auth[WHOLE + u], 1.0, 0.0
+            ).astype(BF16)
 
     def pair(to, p):
         return to * SIDE + 2 * p
@@ -407,13 +410,22 @@
     def half(h):
         return slice(h * HALF, h * HALF + HALF)
 
+    def late_rows(h, owner):
+        span = pl.ds(pl.multiple_of(owner * OWN, OWN), OWN)
+        acc[span, half(h)] += jnp.dot(late_hot[span, :], late_recv[h], **DOTS)
+
     def rel_first(h):
-        for d in range(2):
-            far_send[h, d] = acc[rows_of(lax.rem(q + 2, REL), d), half(h)].astype(BF16)
+        each(range(LATE), lambda i: late_copy(h, i).wait_recv())
+        across = lax.rem(q + 2, REL)
+        late_rows(h, across)
+        for d in range(2):
+            far_send[h, d] = acc[rows_of(across, d), half(h)].astype(BF16)
             far_copy(h, d).start()
         for d in range(2):
+            late_rows(h, towards(d))
             near_send[h, d, 1 - d] = acc[rows_of(towards(d), 1 - d), half(h)].astype(BF16)
             near_copy(h, d, 1 - d).start()
+        late_rows(h, q)
 
     def rel_second(h):
         for d in range(2):
@@ -431,18 +443,14 @@
                 + near_recv[h, 0, p].astype(F32) + near_recv[h, 1, p].astype(F32)
             )
 
+    loop(0, GROUP // 256, hot_rows)
     scatter(3)
     scatter(4)
     for i in range(3):
         scatter(i)
-    for i in range(LATE // PER_SCAT):
-        scatter_late(0, i)
     rel_first(0)
-    scatter_late(1, 0)
     rel_second(0)
     a_first()
-    for i in range(1, LATE // PER_SCAT):
-        scatter_late(1, i)
     rel_first(1)
     a_second()
     rel_last(0)
@@ -506,6 +514,7 @@
             pltpu.VMEM(whole, BF16),
             pltpu.VMEM(late, BF16),
             pltpu.VMEM(late, BF16),
+            pltpu.VMEM((GROUP, LATE * SLOTS), BF16),
             pltpu.VMEM((NODES, 1, SLOTS), jnp.int32),
             pltpu.VMEM((GROUP, AUTH_W), F32),
             pltpu.VMEM((AUTH_W, OUT_W), F32),

time: 59.7 us -> 57 us (0.955)
  Pallas kernels: 58.8 us -> 56.1 us
    pallas_call x1, Pallas kernels: 56.9 us -> 54.2 us  [on_device(): pl.pallas_call(kernel, out_shape=(jax.ShapeDtypeStruct((OWN, AUTH_W), F32...]
where the time goes in v5:
time: 57 us; the launch traced here: 56.8 us
  Pallas kernels  56.1 us (98%)
  between operations  0.64 us (1%)
    pallas_call x1, Pallas kernels, on_device(): pl.pallas_call(kernel, out_shape=(jax.ShapeDtypeStruct((OWN, AUTH_W), F32...  54.2 us
    pallas_call x1, Pallas kernels, on_device(): pl.pallas_call(hand_over, out_shape=tuple((jax.ShapeDtypeStruct(v.shape,...  1.9 us

profile of v5, /device:TPU:0, one launch (start us, length us, event | category | flops | bytes accessed | tf_op | source)
XLA Modules:
  0.0 56.8 jit_solution(15457100808209422002)
XLA Ops:
  0.6 54.2 %shard_map.94 = (f32[512,256]{1,0:T(8,128)}, f32[8,1024]{1,0:T(8,128)}, f32[24,256]{1,0:T(8,128)}) custom-call(s32[32,128]{1,0:T(8,128)} %bitcast.8, s32[32]{0:T(128)} %bitcast.10, s32[32,1,128]{2,1,0:T(1,128)} %bitcast.9, bf16[256,1024]{1,0:T(8,128)(2,1)} %bitcast.7, bf16[4608,1024]{1,0:T(8,128)(2,1)} %go_hbm.1, bf16[4608,768]{1,0:T(8,128)(2,1)} %pf_hbm.1, ...), custom_call_target="tpu_custom_call" | custom-call | tf_op jit(solution)/shard_map/pallas_call | solution.py:495
  54.9 1.9 %shard_map.95 = (f32[512,256]{1,0:T(8,128)}, f32[8,1024]{1,0:T(8,128)}, f32[24,256]{1,0:T(8,128)}) custom-call(f32[512,256]{1,0:T(8,128)} %get-tuple-element.9.a, f32[8,1024]{1,0:T(8,128)} %get-tuple-element.10.b, f32[24,256]{1,0:T(8,128)} %get-tuple-element.11.c), custom_call_target="tpu_custom_call" | custom-call | tf_op jit(solution)/shard_map/pallas_call | solution.py:549

commit v6 on v5

--- a/solution.py
+++ b/solution.py
@@ -16,9 +16,9 @@
 SLOTS, GROUP, OWN = 128, 2048, 512
 CHUNK = 768
 CHUNKS = PAPERS // CHUNK
-STEP = 384
+STEP = 768
 STEPS = PAPERS // STEP
-AHEAD = 5
+AHEAD = 3
 PIECE = 112
 PER_SCAT = 4
 SCAT_ROWS = 1024
@@ -259,11 +259,10 @@
         relay_copy(t).wait_recv()
         msg_copy(t).start()
 
-    loop(0, 2, grads_step)
+    each(range(LATE), lambda i: late_copy(0, i).start())
     each(RELAYED, forward)
-    for h in range(2):
-        each(range(LATE), lambda i: late_copy(h, i).start())
-    loop(2, CHUNKS, grads_step)
+    each(range(LATE), lambda i: late_copy(1, i).start())
+    loop(0, CHUNKS, grads_step)
 
     sacc_t = sacc[...].T
     for n in range(NODES):

time: 57 us -> 59.5 us (1.044)
  Pallas kernels: 56.1 us -> 58.7 us
    pallas_call x1, Pallas kernels: 54.2 us -> 56.8 us  [on_device(): pl.pallas_call(kernel, out_shape=(jax.ShapeDtypeStruct((OWN, AUTH_W), F32...]
where the time goes in v6:
time: 59.5 us; the launch traced here: 59.3 us
  Pallas kernels  58.7 us (99%)
  between operations  0.64 us (1%)
    pallas_call x1, Pallas kernels, on_device(): pl.pallas_call(kernel, out_shape=(jax.ShapeDtypeStruct((OWN, AUTH_W), F32...  56.8 us
    pallas_call x1, Pallas kernels, on_device(): pl.pallas_call(hand_over, out_shape=tuple((jax.ShapeDtypeStruct(v.shape,...  1.9 us

profile of v6, /device:TPU:0, one launch (start us, length us, event | category | flops | bytes accessed | tf_op | source)
XLA Modules:
  0.0 59.3 jit_solution(10974406800840183156)
XLA Ops:
  0.6 56.8 %shard_map.94 = (f32[512,256]{1,0:T(8,128)}, f32[8,1024]{1,0:T(8,128)}, f32[24,256]{1,0:T(8,128)}) custom-call(s32[32,128]{1,0:T(8,128)} %bitcast.8, s32[32]{0:T(128)} %bitcast.10, s32[32,1,128]{2,1,0:T(1,128)} %bitcast.9, bf16[256,1024]{1,0:T(8,128)(2,1)} %bitcast.7, bf16[4608,1024]{1,0:T(8,128)(2,1)} %go_hbm.1, bf16[4608,768]{1,0:T(8,128)(2,1)} %pf_hbm.1, ...), custom_call_target="tpu_custom_call" | custom-call | tf_op jit(solution)/shard_map/pallas_call | solution.py:494
  57.4 1.9 %shard_map.95 = (f32[512,256]{1,0:T(8,128)}, f32[8,1024]{1,0:T(8,128)}, f32[24,256]{1,0:T(8,128)}) custom-call(f32[512,256]{1,0:T(8,128)} %get-tuple-element.9.a, f32[8,1024]{1,0:T(8,128)} %get-tuple-element.10.b, f32[24,256]{1,0:T(8,128)} %get-tuple-element.11.c), custom_call_target="tpu_custom_call" | custom-call | tf_op jit(solution)/shard_map/pallas_call | solution.py:548

commit v7 on v5

--- a/solution.py
+++ b/solution.py
@@ -158,21 +158,23 @@
     w_copy.wait()
     wt[...] = w[...].astype(F32).T.astype(BF16)
 
+    def shared(src, dst, send_sem, recv_sem, to):
+        return pltpu.make_async_remote_copy(
+            src_ref=src, dst_ref=dst, send_sem=send_sem, recv_sem=recv_sem,
+            device_id={"nodes": to}, device_id_type=MESH,
+        )
+
     def remote(src, dst, sems, i, to):
-        return pltpu.make_async_remote_copy(
-            src_ref=src, dst_ref=dst, send_sem=sems[0].at[i], recv_sem=sems[1].at[i],
-            device_id={"nodes": to}, device_id_type=MESH,
-        )
+        return shared(src, dst, sems[0].at[i], sems[1].at[i], to)
+
+    def wait_bytes(ref, sem):
+        pltpu.make_async_copy(ref, ref, sem).wait()
 
     def auth_copy(t):
-        return pltpu.make_async_remote_copy(
-            src_ref=authors.at[at.peer(t)], dst_ref=auth.at[t], send_sem=au_s, recv_sem=au_r,
-            device_id={"nodes": at.peer(t)}, device_id_type=MESH,
-        )
+        return shared(authors.at[at.peer(t)], auth.at[t], au_s, au_r, at.peer(t))
 
     def all_authors(sem):
-        rows_of_all = auth.at[0:NODES - 1]
-        pltpu.make_async_copy(rows_of_all, rows_of_all, sem).wait()
+        wait_bytes(auth.at[0:NODES - 1], sem)
 
     def back_step(k):
         g_copy(k).wait()
@@ -192,19 +194,21 @@
 
     def relay_copy(t):
         i = RELAYED.index(t)
-        return remote(send.at[block(t)], relay.at[block(i)], (rl_s, rl_r), i, node(*first_hop(t)))
+        return shared(
+            send.at[block(t)], relay.at[block(i)], rl_s, rl_r.at[i], node(*first_hop(t))
+        )
 
     def msg_copy(t):
         if t in RELAYED:
             source, to = relay.at[block(RELAYED.index(t))], node(*second_hop(t))
         else:
             source, to = send.at[block(t)], at.peer(t)
-        return remote(source, recv.at[block(t)], (ms_s, ms_r), t, to)
+        return shared(source, recv.at[block(t)], ms_s, ms_r.at[t], to)
 
     def late_copy(h, i):
-        return remote(
+        return shared(
             late_send.at[h, block(i)], late_recv.at[h, block(i)],
-            (lt_s, lt_r), h * LATE + i, at.peer(WHOLE + i),
+            lt_s.at[h], lt_r.at[h], at.peer(WHOLE + i),
         )
 
     def gather(b):
@@ -259,11 +263,11 @@
         relay_copy(t).wait_recv()
         msg_copy(t).start()
 
-    loop(0, 2, grads_step)
+    loop(0, 3, grads_step)
     each(RELAYED, forward)
     for h in range(2):
         each(range(LATE), lambda i: late_copy(h, i).start())
-    loop(2, CHUNKS, grads_step)
+    loop(3, CHUNKS, grads_step)
 
     sacc_t = sacc[...].T
     for n in range(NODES):
@@ -415,7 +419,7 @@
         acc[span, half(h)] += jnp.dot(late_hot[span, :], late_recv[h], **DOTS)
 
     def rel_first(h):
-        each(range(LATE), lambda i: late_copy(h, i).wait_recv())
+        wait_bytes(late_recv.at[h], lt_r.at[h])
         across = lax.rem(q + 2, REL)
         late_rows(h, across)
         for d in range(2):
@@ -457,10 +461,10 @@
     rel_second(1)
     b_first()
     all_authors(au_s)
-    each(RELAYED, lambda t: relay_copy(t).wait_send())
-    each(RELAYED + DIRECT, lambda t: msg_copy(t).wait_send())
+    wait_bytes(relay, rl_s)
+    wait_bytes(recv.at[0:(WHOLE - 1) * SLOTS], ms_s)
     for h in range(2):
-        each(range(LATE), lambda i: late_copy(h, i).wait_send())
+        wait_bytes(late_send.at[h], lt_s.at[h])
     core_copy.wait_send()
     b_last()
     rel_last(1)
@@ -534,8 +538,8 @@
             pltpu.VMEM((2, 2, 2, PART, HALF), BF16),
             pltpu.VMEM((2, 2, 2, PART, HALF), BF16),
             dma, dma((STEPS,)), dma((CHUNKS,)), dma((CHUNKS,)),
-            dma, dma, dma((WHOLE,)), dma((WHOLE,)),
-            dma((len(RELAYED),)), dma((len(RELAYED),)), dma((2 * LATE,)), dma((2 * LATE,)),
+            dma, dma, dma, dma((WHOLE,)),
+            dma, dma((len(RELAYED),)), dma((2,)), dma((2,)),
             dma, dma, dma((2,)), dma((2,)), dma((4,)), dma((4,)), dma((3,)), dma((3,)),
             dma((2, 2)), dma((2, 2)), dma((2, 2, 2)), dma((2, 2, 2)),
         ],

time: 57 us -> 57 us (level)
  no operation moved by 1% of the time
where the time goes in v7:
time: 57 us; the launch traced here: 56.8 us
  Pallas kernels  56.2 us (99%)
  between operations  0.64 us (1%)
    pallas_call x1, Pallas kernels, on_device(): pl.pallas_call(kernel, out_shape=(jax.ShapeDtypeStruct((OWN, AUTH_W), F32...  54.3 us
    pallas_call x1, Pallas kernels, on_device(): pl.pallas_call(hand_over, out_shape=tuple((jax.ShapeDtypeStruct(v.shape,...  1.9 us

profile of v7, /device:TPU:0, one launch (start us, length us, event | category | flops | bytes accessed | tf_op | source)
XLA Modules:
  0.0 56.8 jit_solution(1131130410718351673)
XLA Ops:
  0.6 54.3 %shard_map.94 = (f32[512,256]{1,0:T(8,128)}, f32[8,1024]{1,0:T(8,128)}, f32[24,256]{1,0:T(8,128)}) custom-call(s32[32,128]{1,0:T(8,128)} %bitcast.8, s32[32]{0:T(128)} %bitcast.10, s32[32,1,128]{2,1,0:T(1,128)} %bitcast.9, bf16[256,1024]{1,0:T(8,128)(2,1)} %bitcast.7, bf16[4608,1024]{1,0:T(8,128)(2,1)} %go_hbm.1, bf16[4608,768]{1,0:T(8,128)(2,1)} %pf_hbm.1, ...), custom_call_target="tpu_custom_call" | custom-call | tf_op jit(solution)/shard_map/pallas_call | solution.py:499
  54.9 1.9 %shard_map.95 = (f32[512,256]{1,0:T(8,128)}, f32[8,1024]{1,0:T(8,128)}, f32[24,256]{1,0:T(8,128)}) custom-call(f32[512,256]{1,0:T(8,128)} %get-tuple-element.9.a, f32[8,1024]{1,0:T(8,128)} %get-tuple-element.10.b, f32[24,256]{1,0:T(8,128)} %get-tuple-element.11.c), custom_call_target="tpu_custom_call" | custom-call | tf_op jit(solution)/shard_map/pallas_call | solution.py:553

commit v8 on v7

--- a/solution.py
+++ b/solution.py
@@ -16,9 +16,9 @@
 SLOTS, GROUP, OWN = 128, 2048, 512
 CHUNK = 768
 CHUNKS = PAPERS // CHUNK
-STEP = 384
+STEP = 768
 STEPS = PAPERS // STEP
-AHEAD = 5
+AHEAD = 3
 PIECE = 112
 PER_SCAT = 4
 SCAT_ROWS = 1024

time: 57 us -> 56.3 us (0.988)
  Pallas kernels: 56.2 us -> 55.4 us
    pallas_call x1, Pallas kernels: 54.3 us -> 53.5 us  [on_device(): pl.pallas_call(kernel, out_shape=(jax.ShapeDtypeStruct((OWN, AUTH_W), F32...]
where the time goes in v8:
time: 56.3 us; the launch traced here: 56.1 us
  Pallas kernels  55.4 us (98%)
  between operations  0.64 us (1%)
    pallas_call x1, Pallas kernels, on_device(): pl.pallas_call(kernel, out_shape=(jax.ShapeDtypeStruct((OWN, AUTH_W), F32...  53.5 us
    pallas_call x1, Pallas kernels, on_device(): pl.pallas_call(hand_over, out_shape=tuple((jax.ShapeDtypeStruct(v.shape,...  1.9 us

profile of v8, /device:TPU:0, one launch (start us, length us, event | category | flops | bytes accessed | tf_op | source)
XLA Modules:
  0.0 56.1 jit_solution(2342069887734457056)
XLA Ops:
  0.6 53.5 %shard_map.94 = (f32[512,256]{1,0:T(8,128)}, f32[8,1024]{1,0:T(8,128)}, f32[24,256]{1,0:T(8,128)}) custom-call(s32[32,128]{1,0:T(8,128)} %bitcast.8, s32[32]{0:T(128)} %bitcast.10, s32[32,1,128]{2,1,0:T(1,128)} %bitcast.9, bf16[256,1024]{1,0:T(8,128)(2,1)} %bitcast.7, bf16[4608,1024]{1,0:T(8,128)(2,1)} %go_hbm.1, bf16[4608,768]{1,0:T(8,128)(2,1)} %pf_hbm.1, ...), custom_call_target="tpu_custom_call" | custom-call | tf_op jit(solution)/shard_map/pallas_call | solution.py:499
  54.2 1.9 %shard_map.95 = (f32[512,256]{1,0:T(8,128)}, f32[8,1024]{1,0:T(8,128)}, f32[24,256]{1,0:T(8,128)}) custom-call(f32[512,256]{1,0:T(8,128)} %get-tuple-element.9.a, f32[8,1024]{1,0:T(8,128)} %get-tuple-element.10.b, f32[24,256]{1,0:T(8,128)} %get-tuple-element.11.c), custom_call_target="tpu_custom_call" | custom-call | tf_op jit(solution)/shard_map/pallas_call | solution.py:553

commit v9 on v8

--- a/solution.py
+++ b/solution.py
@@ -263,11 +263,11 @@
         relay_copy(t).wait_recv()
         msg_copy(t).start()
 
-    loop(0, 3, grads_step)
+    loop(0, 4, grads_step)
     each(RELAYED, forward)
     for h in range(2):
         each(range(LATE), lambda i: late_copy(h, i).start())
-    loop(3, CHUNKS, grads_step)
+    loop(4, CHUNKS, grads_step)
 
     sacc_t = sacc[...].T
     for n in range(NODES):

time: 56.3 us -> 57.2 us (1.016)
  Pallas kernels: 55.4 us -> 56.4 us
    pallas_call x1, Pallas kernels: 53.5 us -> 54.5 us  [on_device(): pl.pallas_call(kernel, out_shape=(jax.ShapeDtypeStruct((OWN, AUTH_W), F32...]
where the time goes in v9:
time: 57.2 us; the launch traced here: 57 us
  Pallas kernels  56.4 us (99%)
  between operations  0.64 us (1%)
    pallas_call x1, Pallas kernels, on_device(): pl.pallas_call(kernel, out_shape=(jax.ShapeDtypeStruct((OWN, AUTH_W), F32...  54.5 us
    pallas_call x1, Pallas kernels, on_device(): pl.pallas_call(hand_over, out_shape=tuple((jax.ShapeDtypeStruct(v.shape,...  1.9 us

profile of v9, /device:TPU:0, one launch (start us, length us, event | category | flops | bytes accessed | tf_op | source)
XLA Modules:
  0.0 57.0 jit_solution(1868950955874489471)
XLA Ops:
  0.6 54.5 %shard_map.94 = (f32[512,256]{1,0:T(8,128)}, f32[8,1024]{1,0:T(8,128)}, f32[24,256]{1,0:T(8,128)}) custom-call(s32[32,128]{1,0:T(8,128)} %bitcast.8, s32[32]{0:T(128)} %bitcast.10, s32[32,1,128]{2,1,0:T(1,128)} %bitcast.9, bf16[256,1024]{1,0:T(8,128)(2,1)} %bitcast.7, bf16[4608,1024]{1,0:T(8,128)(2,1)} %go_hbm.1, bf16[4608,768]{1,0:T(8,128)(2,1)} %pf_hbm.1, ...), custom_call_target="tpu_custom_call" | custom-call | tf_op jit(solution)/shard_map/pallas_call | solution.py:499
  55.1 1.9 %shard_map.95 = (f32[512,256]{1,0:T(8,128)}, f32[8,1024]{1,0:T(8,128)}, f32[24,256]{1,0:T(8,128)}) custom-call(f32[512,256]{1,0:T(8,128)} %get-tuple-element.9.a, f32[8,1024]{1,0:T(8,128)} %get-tuple-element.10.b, f32[24,256]{1,0:T(8,128)} %get-tuple-element.11.c), custom_call_target="tpu_custom_call" | custom-call | tf_op jit(solution)/shard_map/pallas_call | solution.py:553
